TPU v7x, 32 devices: a whole 2x2x4 slice. The times are simulated.
32 devices in a mesh: seq: 16 (over z, y, x), head: 2 (over core).
Axes of the slice: x: 2, y: 2, z: 4, core: 2. Of those that a mesh axis runs over, the one named last changes fastest.
Arguments:
- tokens: bfloat16 [2, 4096, 1024], P(None, 'seq'), may hold values from -6 to 6
- w_query: bfloat16 [1024, 512], P(None, 'head'), may hold values from -0.1875 to 0.1875
- w_key: bfloat16 [1024, 512], P(None, 'head'), may hold values from -0.1875 to 0.1875
- w_value: bfloat16 [1024, 1024], P(None, 'head'), may hold values from -0.1875 to 0.1875
- w_outgate: bfloat16 [1024, 1024], P(None, 'head'), may hold values from -0.1875 to 0.1875
- w_gates: bfloat16 [2, 1024, 4], P(None, None, 'head'), may hold values from -0.1875 to 0.1875
- gate_bias: float32 [2, 4], P(None, 'head'), may hold values from -6.5 to 11.5
- conv_query: float32 [4, 512], P(None, 'head'), may hold values from -3 to 3
- conv_key: float32 [4, 512], P(None, 'head'), may hold values from -3 to 3
- conv_value: float32 [4, 1024], P(None, 'head'), may hold values from -3 to 3
- out_gain: float32 [256], replicated, may hold values from 0.5 to 1.5
- w_out: bfloat16 [1024, 1024], P('head'), may hold values from -0.375 to 0.375
- mix_gain: float32 [1024], replicated, may hold values from 0.5 to 1.5
- ffn_gain: float32 [1024], replicated, may hold values from 0.5 to 1.5
- w_gate: bfloat16 [1024, 2816], P(None, 'head'), may hold values from -0.1875 to 0.1875
- w_up: bfloat16 [1024, 2816], P(None, 'head'), may hold values from -0.1875 to 0.1875
- w_down: bfloat16 [2816, 1024], P('head'), may hold values from -0.15625 to 0.15625
- cotangent: bfloat16 [2, 4096, 1024], P(None, 'seq'), may hold values from -6 to 6
Outputs:
- result: bfloat16 [2, 4096, 1024], P(None, 'seq')
- grad_input: float32 [2, 4096, 1024], P(None, 'seq')
- grad_w_query: float32 [1024, 512], P('seq', 'head')
- grad_w_key: float32 [1024, 512], P('seq', 'head')
- grad_w_value: float32 [1024, 1024], P('seq', 'head')
- grad_w_outgate: float32 [1024, 1024], P('seq', 'head')
- grad_w_gates: float32 [2, 1024, 4], P(None, 'seq', 'head')
- grad_gate_bias: float32 [2, 4], P(None, 'head')
- grad_conv_query: float32 [4, 512], P(None, 'head')
- grad_conv_key: float32 [4, 512], P(None, 'head')
- grad_conv_value: float32 [4, 1024], P(None, 'head')
- grad_out_gain: float32 [256], replicated
- grad_w_out: float32 [1024, 1024], P('head', 'seq')
- grad_mix_gain: float32 [1024], P('seq')
- grad_ffn_gain: float32 [1024], P('seq')
- grad_w_gate: float32 [1024, 2816], P('seq', 'head')
- grad_w_up: float32 [1024, 2816], P('seq', 'head')
- grad_w_down: float32 [2816, 1024], P('head', 'seq')
All inputs are finite; a program needn't handle non-finite values.
Results may differ from a plain program's by a relative error of at most 0.013.
Values may be sent and summed in bfloat16 or wider, within the bound.
No kernel may reach another device: no remote copies, remote signals or barrier semaphores. Data moves between devices by JAX's collectives and lax.ppermute only.
A program may use at most 448 MiB of HBM per device.

v0:
```python
import jax
import jax.numpy as jnp
from jax import lax
from jax.sharding import PartitionSpec as P

DK = 128
DV = 256
CONV = 4
GROUP = 64


HIGHEST = lax.Precision.HIGHEST


def passed_along(block, axis, distance):
    devices = range(lax.axis_size(axis))
    route = [(i - distance, i) for i in devices if i - distance in devices]
    return lax.ppermute(block, axis, route)


def entering(value, axis, join, neutral, backward):
    count, mine = (lax.axis_size(axis), lax.axis_index(axis))
    pieces = jax.tree.map(lambda part: lax.all_gather(part, axis), value)
    if backward:
        pieces = jax.tree.map(lambda part: part[::-1], pieces)
        mine = count - 1 - mine
    running = jax.tree.map(
        lambda part, zero: jnp.full_like(part, 0) + jnp.asarray(zero, part.dtype), value, neutral
    )

    def lap(position, running):
        longer = join(running, jax.tree.map(lambda part: part[position], pieces))
        return jax.tree.map(lambda new, old: jnp.where(position < mine, new, old), longer, running)

    return lax.fori_loop(0, count - 1, lap, running)


def rms_scale(values, epsilon):
    return lax.rsqrt(jnp.mean(values * values, axis=-1, keepdims=True) + epsilon)


def norm_apply(values, gain):
    return values * rms_scale(values, 1e-06) * gain


def inverse_unit(strict_lower):
    block_size = strict_lower.shape[-1]
    identity_map = jnp.eye(block_size, dtype=strict_lower.dtype)
    power = -strict_lower
    inverse = identity_map + power
    for level in range(1, block_size.bit_length() - 1):
        power = jnp.matmul(power, power, precision=HIGHEST)
        inverse = jnp.matmul(inverse, identity_map + power, precision=HIGHEST)
    return inverse


def group_step(carry_state, block):
    queries, keys_unit, values, beta_rate, logdecay = block
    block_size = keys_unit.shape[1]
    positions = jnp.arange(block_size)
    strict = (positions[:, None] > positions[None, :]).astype(carry_state.dtype)
    within = (positions[:, None] >= positions[None, :]).astype(carry_state.dtype)
    cumulative = jnp.cumsum(jnp.swapaxes(logdecay, 1, 2), axis=-1)
    beta_row = jnp.swapaxes(beta_rate, 1, 2)
    decays = (
        jnp.exp(jnp.minimum(cumulative[..., :, None] - cumulative[..., None, :], 0.0))
        * beta_row[..., None, :]
    )
    strict_lower = (
        jnp.einsum("sthd,suhd->shtu", keys_unit, keys_unit, precision=HIGHEST) * decays * strict
    )
    growth = jnp.exp(cumulative)[..., None]
    carried = jnp.einsum("sthd,shde->shte", keys_unit, carry_state, precision=HIGHEST)
    fresh_values = jnp.matmul(
        inverse_unit(strict_lower), jnp.swapaxes(values, 1, 2) - growth * carried, precision=HIGHEST
    )
    scores = jnp.einsum("sthd,suhd->shtu", queries, keys_unit, precision=HIGHEST) * decays * within
    output = growth * jnp.einsum("sthd,shde->shte", queries, carry_state, precision=HIGHEST)
    output = output + jnp.matmul(scores, fresh_values, precision=HIGHEST)
    tail_weight = jnp.exp(cumulative[..., -1:] - cumulative) * beta_row
    new_state = jnp.exp(cumulative[..., -1])[..., None, None] * carry_state
    new_state = new_state + jnp.einsum(
        "sht,sthd,shte->shde", tail_weight, keys_unit, fresh_values, precision=HIGHEST
    )
    return (new_state, jnp.swapaxes(output, 1, 2))


def run_groups(carry_state, queries, keys_unit, values, beta_rate, logdecay):

    def to_blocks(field):
        count = field.shape[1] // GROUP
        return jnp.swapaxes(field.reshape((field.shape[0], count, GROUP) + field.shape[2:]), 0, 1)

    blocks = tuple(
        (to_blocks(field) for field in (queries, keys_unit, values, beta_rate, logdecay))
    )
    final_state, outputs = lax.scan(group_step, carry_state, blocks)
    outputs = jnp.swapaxes(outputs, 0, 1)
    return (
        outputs.reshape(
            (outputs.shape[0], outputs.shape[1] * outputs.shape[2]) + outputs.shape[3:]
        ),
        final_state,
    )


def short_conv(extended, kernel):
    length = extended.shape[1] - CONV + 1
    summed = kernel[0] * extended[:, 0:length]
    for offset in range(1, CONV):
        summed = summed + kernel[offset] * extended[:, offset : offset + length]
    return jax.nn.silu(summed)


def unit_rows(field):
    return field * lax.rsqrt(jnp.sum(field * field, axis=-1, keepdims=True) + 1e-06)


def mixer_inputs(ext_q, ext_k, ext_v, gates, conv_query, conv_key, conv_value, gate_bias):
    conv_q = short_conv(ext_q, conv_query)
    head_shape = conv_q.shape[:2] + (conv_q.shape[2] // DK, DK)
    queries = unit_rows(conv_q.reshape(head_shape)) * DK ** (-0.5)
    keys_unit = unit_rows(short_conv(ext_k, conv_key).reshape(head_shape))
    conv_v = short_conv(ext_v, conv_value)
    values = conv_v.reshape(conv_v.shape[:2] + (conv_v.shape[2] // DV, DV))
    beta_rate = jax.nn.sigmoid(gates[:, :, 0] + gate_bias[0])
    logdecay = jax.nn.log_sigmoid(gates[:, :, 1] + gate_bias[1])
    return (queries, keys_unit, values, beta_rate, logdecay)


def gated_norm(output, proj_g, out_gain):
    gate_value = proj_g.reshape(output.shape)
    normed = output * rms_scale(output, 1e-05) * out_gain * jax.nn.silu(gate_value)
    return normed.reshape(proj_g.shape)


def compose(earlier, later):
    early_map, early_shift = earlier
    late_map, late_shift = later
    joined_map = jnp.matmul(late_map, early_map, precision=HIGHEST)
    joined_shift = jnp.matmul(late_map, early_shift, precision=HIGHEST) + late_shift
    return (joined_map, joined_shift)


def product(left, right):
    return jnp.einsum("spa,ab->spb", left, right, preferred_element_type=jnp.float32)


def weight_grad(left, right):
    return jnp.einsum("spa,spb->ab", left, right, preferred_element_type=jnp.float32)


def back_product(grad_rows, weight):
    return jnp.einsum("spb,ab->spa", grad_rows, weight, preferred_element_type=jnp.float32)


def on_device(
    tokens,
    w_query,
    w_key,
    w_value,
    w_outgate,
    w_gates,
    gate_bias,
    conv_query,
    conv_key,
    conv_value,
    out_gain,
    w_out,
    mix_gain,
    ffn_gain,
    w_gate,
    w_up,
    w_down,
    cotangent,
):
    inputs = tokens.astype(jnp.float32)
    mixed_full, first_norm_back = jax.vjp(norm_apply, inputs, mix_gain)
    mixed = mixed_full.astype(jnp.bfloat16)
    proj_q = product(mixed, w_query).astype(jnp.bfloat16)
    proj_k = product(mixed, w_key).astype(jnp.bfloat16)
    proj_v = product(mixed, w_value).astype(jnp.bfloat16)
    proj_g = product(mixed, w_outgate)
    gates = jnp.einsum("spd,cdh->spch", mixed, w_gates, preferred_element_type=jnp.float32)
    width_q = proj_q.shape[2]
    width_k = proj_k.shape[2]
    edge_rows = CONV - 1
    outgoing = jnp.concatenate(
        [proj_q[:, -edge_rows:], proj_k[:, -edge_rows:], proj_v[:, -edge_rows:]], axis=2
    )
    incoming = passed_along(outgoing, "seq", 1)
    ext_q = jnp.concatenate([incoming[..., :width_q], proj_q], axis=1).astype(jnp.float32)
    ext_k = jnp.concatenate([incoming[..., width_q : width_q + width_k], proj_k], axis=1).astype(
        jnp.float32
    )
    ext_v = jnp.concatenate([incoming[..., width_q + width_k :], proj_v], axis=1).astype(
        jnp.float32
    )
    mixer_vals, prepare_back = jax.vjp(
        mixer_inputs, ext_q, ext_k, ext_v, gates, conv_query, conv_key, conv_value, gate_bias
    )
    queries, keys_unit, values, beta_rate, logdecay = mixer_vals
    seqs_here = keys_unit.shape[0]
    heads_here = keys_unit.shape[2]
    identity_map = jnp.broadcast_to(jnp.eye(DK, dtype=jnp.float32), (seqs_here, heads_here, DK, DK))
    zero_shift = jnp.zeros((seqs_here, heads_here, DK, DV), jnp.float32)
    start_state = jnp.concatenate([identity_map, zero_shift], axis=-1)
    widened = jnp.concatenate([jnp.zeros(values.shape[:3] + (DK,), jnp.float32), values], axis=-1)
    unused_out, piece_ends = run_groups(
        start_state, queries, keys_unit, widened, beta_rate, logdecay
    )
    piece_map = piece_ends[..., :DK]
    piece_shift = piece_ends[..., DK:]
    entry_map, entry_state = entering(
        (piece_map, piece_shift), "seq", compose, (identity_map, zero_shift), False
    )
    recurrence, recur_back = jax.vjp(
        run_groups, entry_state, queries, keys_unit, values, beta_rate, logdecay
    )
    output = recurrence[0]
    gated_full, gate_norm_back = jax.vjp(gated_norm, output, proj_g, out_gain)
    gated = gated_full.astype(jnp.bfloat16)
    attn_out = lax.psum(product(gated, w_out), "head")
    resid = inputs + attn_out
    normed_full, second_norm_back = jax.vjp(norm_apply, resid, ffn_gain)
    normed = normed_full.astype(jnp.bfloat16)
    gate_value = product(normed, w_gate)
    up_value = product(normed, w_up)
    sigmoid_gate = jax.nn.sigmoid(gate_value)
    activated = gate_value * sigmoid_gate
    hidden = (activated * up_value).astype(jnp.bfloat16)
    ffn_out = lax.psum(product(hidden, w_down).astype(jnp.bfloat16), "head").astype(jnp.float32)
    result = (resid + ffn_out).astype(jnp.bfloat16)
    grad_w_down = weight_grad(hidden, cotangent)
    grad_hidden = back_product(cotangent, w_down)
    grad_gate = (
        grad_hidden * up_value * (sigmoid_gate + gate_value * sigmoid_gate * (1.0 - sigmoid_gate))
    ).astype(jnp.bfloat16)
    grad_up = (grad_hidden * activated).astype(jnp.bfloat16)
    grad_w_gate = weight_grad(normed, grad_gate)
    grad_w_up = weight_grad(normed, grad_up)
    part_normed = back_product(grad_gate, w_gate) + back_product(grad_up, w_up)
    grad_normed = lax.psum(part_normed, "head")
    grad_resid_norm, grad_ffn_gain = second_norm_back(grad_normed)
    grad_resid = cotangent.astype(jnp.float32) + grad_resid_norm
    grad_attn = grad_resid.astype(jnp.bfloat16)
    grad_w_out = weight_grad(gated, grad_attn)
    grad_gated = back_product(grad_attn, w_out)
    grad_output, grad_proj_g, grad_out_gain = gate_norm_back(grad_gated)
    first_pass = recur_back((grad_output, jnp.zeros_like(zero_shift)))
    reverse_map = jnp.swapaxes(piece_map, -1, -2)
    exit_map, exit_grad = entering(
        (reverse_map, first_pass[0]), "seq", compose, (identity_map, zero_shift), True
    )
    second_pass = recur_back((jnp.zeros_like(grad_output), exit_grad))
    mixer_grads = tuple(
        (
            first_term + second_term
            for first_term, second_term in zip(first_pass[1:], second_pass[1:])
        )
    )
    (
        grad_ext_q,
        grad_ext_k,
        grad_ext_v,
        grad_gates,
        grad_conv_q,
        grad_conv_k,
        grad_conv_v,
        grad_bias,
    ) = prepare_back(mixer_grads)
    edge_grads = jnp.concatenate(
        [grad_ext_q[:, :edge_rows], grad_ext_k[:, :edge_rows], grad_ext_v[:, :edge_rows]], axis=2
    )
    returned = passed_along(edge_grads, "seq", -1)
    grad_q = (
        grad_ext_q[:, edge_rows:]
        .at[:, -edge_rows:]
        .add(returned[..., :width_q])
        .astype(jnp.bfloat16)
    )
    grad_k = (
        grad_ext_k[:, edge_rows:]
        .at[:, -edge_rows:]
        .add(returned[..., width_q : width_q + width_k])
        .astype(jnp.bfloat16)
    )
    grad_v = (
        grad_ext_v[:, edge_rows:]
        .at[:, -edge_rows:]
        .add(returned[..., width_q + width_k :])
        .astype(jnp.bfloat16)
    )
    grad_g = grad_proj_g.astype(jnp.bfloat16)
    grad_gates_low = grad_gates.astype(jnp.bfloat16)
    grad_w_query = weight_grad(mixed, grad_q)
    grad_w_key = weight_grad(mixed, grad_k)
    grad_w_value = weight_grad(mixed, grad_v)
    grad_w_outgate = weight_grad(mixed, grad_g)
    grad_w_gates = jnp.einsum(
        "spd,spch->cdh", mixed, grad_gates_low, preferred_element_type=jnp.float32
    )
    part_mixed = (
        back_product(grad_q, w_query) + back_product(grad_k, w_key) + back_product(grad_v, w_value)
    )
    part_mixed = part_mixed + back_product(grad_g, w_outgate)
    part_mixed = part_mixed + jnp.einsum(
        "spch,cdh->spd", grad_gates_low, w_gates, preferred_element_type=jnp.float32
    )
    grad_mixed, head_gain = (
        lax.psum(part_mixed.astype(jnp.bfloat16), "head").astype(jnp.float32),
        lax.psum(grad_out_gain.astype(jnp.bfloat16), "head").astype(jnp.float32),
    )
    grad_in_norm, grad_mix_gain = first_norm_back(grad_mixed)
    grad_input = grad_resid + grad_in_norm
    small_sums = lax.psum((grad_conv_q, grad_conv_k, grad_conv_v, grad_bias, head_gain), "seq")
    all_sums = (
        lax.psum_scatter(grad_w_query, "seq", scatter_dimension=0, tiled=True),
        lax.psum_scatter(grad_w_key, "seq", scatter_dimension=0, tiled=True),
        lax.psum_scatter(grad_w_value, "seq", scatter_dimension=0, tiled=True),
        lax.psum_scatter(grad_w_outgate, "seq", scatter_dimension=0, tiled=True),
        lax.psum_scatter(grad_w_gates, "seq", scatter_dimension=1, tiled=True),
        lax.psum_scatter(grad_w_out, "seq", scatter_dimension=1, tiled=True),
        lax.psum_scatter(grad_mix_gain, "seq", scatter_dimension=0, tiled=True),
        lax.psum_scatter(grad_ffn_gain, "seq", scatter_dimension=0, tiled=True),
        lax.psum_scatter(grad_w_gate, "seq", scatter_dimension=0, tiled=True),
        lax.psum_scatter(grad_w_up, "seq", scatter_dimension=0, tiled=True),
        lax.psum_scatter(grad_w_down, "seq", scatter_dimension=1, tiled=True),
    )
    return (
        result,
        grad_input,
        all_sums[0],
        all_sums[1],
        all_sums[2],
        all_sums[3],
        all_sums[4],
        small_sums[3],
        small_sums[0],
        small_sums[1],
        small_sums[2],
        small_sums[4],
        all_sums[5],
        all_sums[6],
        all_sums[7],
        all_sums[8],
        all_sums[9],
        all_sums[10],
    )


def solution(mesh):
    return jax.shard_map(
        on_device,
        mesh=mesh,
        in_specs=(
            P(None, "seq", None),
            P(None, "head"),
            P(None, "head"),
            P(None, "head"),
            P(None, "head"),
            P(None, None, "head"),
            P(None, "head"),
            P(None, "head"),
            P(None, "head"),
            P(None, "head"),
            P(),
            P("head", None),
            P(),
            P(),
            P(None, "head"),
            P(None, "head"),
            P("head", None),
            P(None, "seq", None),
        ),
        out_specs=(
            P(None, "seq", None),
            P(None, "seq", None),
            P("seq", "head"),
            P("seq", "head"),
            P("seq", "head"),
            P("seq", "head"),
            P(None, "seq", "head"),
            P(None, "head"),
            P(None, "head"),
            P(None, "head"),
            P(None, "head"),
            P(),
            P("head", "seq"),
            P("seq"),
            P("seq"),
            P("seq", "head"),
            P("seq", "head"),
            P("head", "seq"),
        ),
        check_vma=False,
    )
```

profile of v0, /device:TPU:0, one launch (start us, length us, event | category | flops | bytes accessed | tf_op | source)
XLA Modules:
  0.0 2148.4 jit_solution(4720888736387065755)
XLA Ops:
  9.5 2.4 convolution_convert_fusion
  13.7 4.8 collective-permute-start
  36.5 41.8 %while.178 = (s32[]{:T(128)}, f32[2,2,128,384]{3,2,1,0:T(8,128)}, f32[4,2,64,2]{2,3,1,0:T(2,128)}, f32[4,2,64,2]{2,3,1,0:T(2,128)}, f32[4,2,64,2,128]{4,2,3,1,0:...) while((s32[]{:T(128)}, f32[2,2,128,384]{3,2,1,0:T(8,128)}, f32[4,2,64,2]{2,3,1,0:T(2,128)}, ...), condition=%wide.region_4.5_spmd, body=%wide.region_2.0_spmd.sunk | while | flops 529334528 | bytes 6657209 | solution.py:97
  43.9 3.0 convolution_add_fusion.62
  54.4 3.0 convolution_add_fusion.62
  64.8 3.0 convolution_add_fusion.62
  75.2 3.0 convolution_add_fusion.62
  84.0 3.0 fusion.523
  93.0 2.8 reshape.730
  95.8 2.4 multiply_reduce_fusion.19
  99.4 2.4 copy.649
  102.8 54.0 %all-gather.9.cloned.1.call-done = f32[32,2,128,128]{3,2,1,0:T(8,128)} async-done(((f32[2,2,128,128]{3,2,1,0:T(8,128)}), f32[32,2,128,128]{3,2,1,0:T(8,128)}) %all-gather.9.cloned.1.call-update) | async-done | bytes 4194320 | tf_op jit(solution)/shard_map/all_gather | solution.py:23
  156.8 114.2 %all-gather.11.cloned.1.call-done = f32[32,2,128,256]{3,2,1,0:T(8,128)} async-done(((f32[2,2,128,256]{3,2,1,0:T(8,128)}), f32[32,2,128,256]{3,2,1,0:T(8,128)}) %all-gather.11.cloned.1.call-update) | async-done | bytes 8388624 | tf_op jit(solution)/shard_map/all_gather | solution.py:23
  271.1 27.4 %while.181 = (s32[]{:T(128)}, f32[2,2,128,256]{3,2,1,0:T(8,128)S(1)}, s32[]{:T(128)}, f32[16,2,2,128,128]{4,3,2,1,0:T(8,128)}, f32[16,2,2,128,256]{4,3,2,1,0:T(8,128)}, /*index=5*/s32[]{:T(128)}, s32[]{:T(128)}) while((s32[]{:T(128)}, f32[2,2,128,256]{3,2,1,0:T(8,128)S(1)}, s32[]{:T(128)}, f32[16,2,2,128,128]{4,3,2,1,0:T(8,128)}, ...), condition=%wide.region_6.7_spmd.clone, body=%wide.region_5.6_spmd.clone.sunk | while | flops 201850880 | bytes 3410527 | solution.py:35
  299.5 203.5 %while.180 = (s32[]{:T(128)}, f32[2,2,128,256]{3,2,1,0:T(8,128)S(1)}, f32[4,2,64,2,256]{4,2,3,1,0:T(8,128)}, f32[4,2,2,64,64]{4,3,2,1,0:T(8,128)}, f32[4,2,2,64,...) while((s32[]{:T(128)}, ...), condition=%wide.region_10.11_spmd.clone.clone, body=%wide.region_8.10_spmd.clone.clone.sunk | while | flops 580281344 | bytes 28029364 | solution.py:97
  506.3 3.1 mul.1441
  509.3 3.1 copy.421
  512.4 3.0 reshape.733
  515.4 4.2 multiply_convert_fusion.4
  522.5 9.1 all-reduce.44.cloned.1.call-start
  531.6 10.5 all-reduce.42.cloned.1.call-done
  550.9 3.9 multiply_convert_fusion.1
  556.6 3.2 fusion.452
  561.7 2.9 reshape.735
  569.2 13.1 all-reduce.44.cloned.1.call-done
  582.4 3.5 multiply_reduce_fusion.1
  590.5 2.9 reshape.734
  593.4 3.2 multiply_reduce_fusion.4
  602.0 238.3 %while.182 = (s32[]{:T(128)}, f32[2,2,128,256]{3,2,1,0:T(8,128)}, f32[4,2,64,2,128]{4,2,0,3,1:T(8,128)}, f32[4,2,64,2,128]{4,2,0,3,1:T(8,128)}, f32[4,2,64,2,256...) while((s32[]{:T(128)}, f32[2,2,128,256]{3,2,1,0:T(8,128)}, ...), condition=%wide.region_27.28_spmd.clone, body=%wide.region_18.27_spmd.clone.sunk | while | flops 1160333056 | bytes 38102536 | solution.py:97
  651.6 2.5 fusion.1149
  659.1 2.4 fusion.1133
  686.2 2.4 fusion.1146
  711.2 2.5 fusion.1149
  718.7 2.4 fusion.1133
  745.8 2.4 fusion.1146
  770.8 2.5 fusion.1149
  778.3 2.4 fusion.1133
  805.4 2.4 fusion.1146
  830.4 2.5 fusion.1149
  837.9 2.4 fusion.1133
  846.7 4.7 rev.6
  851.4 4.2 fusion.455
  857.7 96.8 %all-gather.15.cloned.1.call-done = f32[32,2,128,256]{3,2,1,0:T(8,128)} async-done(((f32[2,2,128,256]{3,2,1,0:T(8,128)}), f32[32,2,128,256]{3,2,1,0:T(8,128)}) %all-gather.15.cloned.1.call-update) | async-done | bytes 8388624 | tf_op jit(solution)/shard_map/all_gather | solution.py:23
  954.5 7.7 rev.7
  962.2 27.5 %while.183 = (s32[]{:T(128)}, f32[2,2,128,256]{3,2,1,0:T(8,128)S(1)}, s32[]{:T(128)}, f32[16,2,2,128,128]{4,3,2,1,0:T(8,128)}, f32[16,2,2,128,256]{4,3,2,1,0:T(8,128)}, /*index=5*/s32[]{:T(128)}, s32[]{:T(128)}) while((s32[]{:T(128)}, f32[2,2,128,256]{3,2,1,0:T(8,128)S(1)}, s32[]{:T(128)}, f32[16,2,2,128,128]{4,3,2,1,0:T(8,128)}, ...), condition=%wide.region_29.30_spmd.clone, body=%wide.region_28.29_spmd.clone.sunk | while | flops 201850880 | bytes 3410527 | solution.py:35
  993.7 214.0 %while.179 = (s32[]{:T(128)}, f32[2,2,128,256]{3,2,1,0:T(8,128)S(1)}, f32[4,2,64,2,128]{4,2,0,3,1:T(8,128)}, f32[4,2,64,2,128]{4,2,0,3,1:T(8,128)}, f32[4,2,64,2...) while((s32[]{:T(128)}, ...), condition=%wide.region_39.40_spmd.clone, body=%wide.region_30.39_spmd.clone.sunk | while | flops 1159677952 | bytes 28398504 | solution.py:97
  1252.3 2.6 reshape.768
  1257.2 2.9 fusion.484
  1263.1 5.6 fusion.451
  1276.0 5.7 convolution_bitcast_fusion.11
  1281.8 5.7 convolution_bitcast_fusion.10
  1288.7 5.6 convolution_bitcast_fusion.9
  1302.2 2.7 psum.78
  1304.9 27.0 %reduce-scatter.28.cloned.1.call-done = f32[64,4]{1,0:T(8,128)} async-done(((f32[1024,4]{1,0:T(8,128)}), f32[64,4]{1,0:T(8,128)}) %reduce-scatter.28.cloned.1.call-update) | async-done | bytes 1040
  1333.5 19.2 all-reduce.46.cloned.1.call-done
  1354.9 77.5 %all-reduce.36 = (f32[2,2]{1,0:T(2,128)}, f32[4,256]{1,0:T(4,128)}, f32[4,256]{1,0:T(4,128)}, f32[4,512]{1,0:T(4,128)}, f32[256]{0:T(256)}, /*index=5*/f32[1024]{0:T(1024)S(1)}, f32[1024]{0:T(1024)S(1)}) all-reduce(f32[2,2]{1,0:T(2,128)S(1)} %pad_add_fusion.9, ...), channel_id=1, replica_groups=mesh['seq'=16,'head'=2] {'seq'}, use_global_device_ids=true, to_apply=%region_51.52 | all-reduce | flops 6404 | bytes 50720 | tf_op jit(solution)/shard_map/psum | solution.py:316
  1433.6 3.3 add_convert_fusion
  1438.8 79.1 %reduce-scatter.18.cloned.1.call-done = f32[64,512]{1,0:T(8,128)} async-done(((f32[1024,512]{1,0:T(8,128)}), f32[64,512]{1,0:T(8,128)}) %reduce-scatter.18.cloned.1.call-update) | async-done | bytes 131088 | tf_op jit(solution)/shard_map/reduce_scatter | solution.py:321
  1517.9 125.9 %reduce-scatter.22.cloned.1.call-done = f32[64,1408]{1,0:T(8,128)} async-done(((f32[1024,1408]{1,0:T(8,128)}), f32[64,1408]{1,0:T(8,128)}) %reduce-scatter.22.cloned.1.call-update) | async-done | bytes 360464 | tf_op jit(solution)/shard_map/reduce_scatter | solution.py:326
  1643.8 129.7 %reduce-scatter.24.cloned.1.call-done = f32[64,1408]{1,0:T(8,128)} async-done(((f32[1024,1408]{1,0:T(8,128)}), f32[64,1408]{1,0:T(8,128)}) %reduce-scatter.24.cloned.1.call-update) | async-done | bytes 360464 | tf_op jit(solution)/shard_map/reduce_scatter | solution.py:327
  1773.5 129.9 %reduce-scatter.26.cloned.1.call-done = f32[1408,64]{0,1:T(8,128)} async-done(((f32[1408,1024]{0,1:T(8,128)}), f32[1408,64]{0,1:T(8,128)}) %reduce-scatter.26.cloned.1.call-update) | async-done | bytes 360464 | tf_op jit(solution)/shard_map/reduce_scatter | solution.py:328
  1903.4 81.3 %reduce-scatter.14.cloned.1.call-done = f32[64,256]{1,0:T(8,128)} async-done(((f32[1024,256]{1,0:T(8,128)}), f32[64,256]{1,0:T(8,128)}) %reduce-scatter.14.cloned.1.call-update) | async-done | bytes 65552 | tf_op jit(solution)/shard_map/reduce_scatter | solution.py:319
  1984.8 76.9 %reduce-scatter.12.cloned.1.call-done = f32[64,256]{1,0:T(8,128)} async-done(((f32[1024,256]{1,0:T(8,128)}), f32[64,256]{1,0:T(8,128)}) %reduce-scatter.12.cloned.1.call-update) | async-done | bytes 65552 | tf_op jit(solution)/shard_map/reduce_scatter | solution.py:318
  2061.6 80.0 %reduce-scatter.16.cloned.1.call-done = f32[64,512]{1,0:T(8,128)} async-done(((f32[1024,512]{1,0:T(8,128)}), f32[64,512]{1,0:T(8,128)}) %reduce-scatter.16.cloned.1.call-update) | async-done | bytes 131088 | tf_op jit(solution)/shard_map/reduce_scatter | solution.py:320
  (1561 shorter events, 860.5 us)
Async XLA Ops:
  7.2 543.7 %copy-start = (bf16[1408,1024]{1,0:T(8,128)(2,1)S(1)}, bf16[1408,1024]{1,0:T(8,128)(2,1)}, u32[]{:S(2)}) copy-start(bf16[1408,1024]{1,0:T(8,128)(2,1)} %param.52) | copy-start | bytes 8650756
  7.2 149.6 %all-gather.9.cloned.1.call-start = ((), (), s32[]{:S(2)}) async-start(), calls=%async_computation.19 | async-start | bytes 4456448 | tf_op jit(solution)/shard_map/all_gather | solution.py:23
  9.5 9.2 copy-start.129
  13.7 9.1 collective-permute-start
  18.6 13.3 copy-start.119
  18.7 13.3 copy-start.121
  18.7 13.3 copy-start.123
  18.7 13.3 copy-start.125
  80.3 190.8 %all-gather.11.cloned.1.call-start = ((), (), s32[]{:S(2)}) async-start(), calls=%async_computation.20 | async-start | bytes 8912896 | tf_op jit(solution)/shard_map/all_gather | solution.py:23
  82.2 459.9 %all-reduce.42.cloned.1.call-start = ((), (), s32[]{:S(2)}) async-start(), calls=%async_computation.9 | async-start | bytes 4194304 | tf_op jit(solution)/shard_map/psum | solution.py:223
  99.3 171.8 %copy-start.111 = (f32[2,256,2]{1,2,0:T(2,128)}, f32[2,256,2]{1,2,0:T(2,128)S(1)}, u32[]{:S(2)}) copy-start(f32[2,256,2]{1,2,0:T(2,128)S(1)} %copy.417) | copy-start | bytes 12292
  522.5 21.8 %copy-start.107 = (f32[1024]{0:T(1024)S(1)}, f32[1024]{0:T(1024)}, u32[]{:S(2)}) copy-start(f32[1024]{0:T(1024)} %param.49) | copy-start | bytes 12292
  522.5 59.8 %all-reduce.44.cloned.1.call-start = ((), (), s32[]{:S(2)}) async-start(), calls=%async_computation.10 | async-start | bytes 4194304 | tf_op jit(solution)/shard_map/psum | solution.py:243
  559.8 286.9 %all-gather.13.cloned.1.call-start = ((), (), s32[]{:S(2)}) async-start(), calls=%async_computation.21 | async-start | bytes 4456448 | tf_op jit(solution)/shard_map/all_gather | solution.py:23
  561.6 392.9 %all-gather.15.cloned.1.call-start = ((), (), s32[]{:S(2)}) async-start(), calls=%async_computation.22 | async-start | bytes 8912896 | tf_op jit(solution)/shard_map/all_gather | solution.py:23
  605.3 7.9 copy-start.17
  616.1 7.9 copy-start.53
  646.1 8.8 copy-start.6
  646.1 8.8 copy-start.18
  647.5 8.9 copy-start.10
  664.6 7.9 copy-start.17
  675.5 7.9 copy-start.53
  705.7 8.7 copy-start.6
  705.7 8.7 copy-start.18
  707.2 8.8 copy-start.10
  724.2 7.9 copy-start.17
  735.0 7.9 copy-start.53
  765.2 8.7 copy-start.6
  765.2 8.7 copy-start.18
  766.7 8.9 copy-start.10
  783.8 7.9 copy-start.17
  794.6 7.9 copy-start.53
  824.9 8.7 copy-start.6
  824.9 8.7 copy-start.18
  826.3 8.9 copy-start.10
  840.3 491.6 %reduce-scatter.28.cloned.1.call-start = ((), (), s32[]{:S(2)}) async-start(), calls=%async_computation.23 | async-start | bytes 557056
  962.2 31.5 %copy-start.7 = (f32[4,2,2,128,256]{4,3,2,1,0:T(8,128)S(1)}, f32[4,2,2,128,256]{4,3,2,1,0:T(8,128)}, u32[]{:S(2)}) copy-start(f32[4,2,2,128,256]{4,3,2,1,0:T(8,128)} %get-tuple-element.5708) | copy-start | bytes 6291460
  993.7 8.7 copy-start.50
  996.3 7.9 copy-start.16
  1005.9 9.0 copy-start.54
  1047.1 8.7 copy-start.50
  1049.7 7.9 copy-start.16
  1051.2 7.6 copy-start.48
  1059.4 9.0 copy-start.54
  1100.5 8.7 copy-start.50
  1103.1 7.9 copy-start.16
  1112.7 9.1 copy-start.54
  1154.0 8.7 copy-start.50
  1156.6 7.9 copy-start.16
  1166.2 9.0 copy-start.54
  1236.4 8.4 copy-start.22
  1247.4 7.5 collective-permute-start.1
  1254.9 97.7 %all-reduce.46.cloned.1.call-start = ((), (), s32[]{:S(2)}) async-start(), calls=%async_computation.24 | async-start | bytes 4194304 | tf_op jit(solution)/shard_map/psum | solution.py:232
  1268.8 170.0 %reduce-scatter.20.cloned.1.call-start = ((), (), s32[]{:S(2)}) async-start(), calls=%async_computation.15 | async-start | bytes 2228224 | tf_op jit(solution)/shard_map/reduce_scatter | solution.py:323
  1272.4 245.5 %reduce-scatter.18.cloned.1.call-start = ((), (), s32[]{:S(2)}) async-start(), calls=%async_computation.14 | async-start | bytes 2228224 | tf_op jit(solution)/shard_map/reduce_scatter | solution.py:321
  1275.9 367.8 %reduce-scatter.22.cloned.1.call-start = ((), (), s32[]{:S(2)}) async-start(), calls=%async_computation.16 | async-start | bytes 6127616 | tf_op jit(solution)/shard_map/reduce_scatter | solution.py:326
  1281.7 491.8 %reduce-scatter.24.cloned.1.call-start = ((), (), s32[]{:S(2)}) async-start(), calls=%async_computation.17 | async-start | bytes 6127616 | tf_op jit(solution)/shard_map/reduce_scatter | solution.py:327
  1287.5 615.9 %reduce-scatter.26.cloned.1.call-start = ((), (), s32[]{:S(2)}) async-start(), calls=%async_computation.18 | async-start | bytes 6127616 | tf_op jit(solution)/shard_map/reduce_scatter | solution.py:328
  1294.3 690.4 %reduce-scatter.14.cloned.1.call-start = ((), (), s32[]{:S(2)}) async-start(), calls=%async_computation.12 | async-start | bytes 1114112 | tf_op jit(solution)/shard_map/reduce_scatter | solution.py:319
  1296.9 764.7 %reduce-scatter.12.cloned.1.call-start = ((), (), s32[]{:S(2)}) async-start(), calls=%async_computation.11 | async-start | bytes 1114112 | tf_op jit(solution)/shard_map/reduce_scatter | solution.py:318
  1298.6 843.0 %reduce-scatter.16.cloned.1.call-start = ((), (), s32[]{:S(2)}) async-start(), calls=%async_computation.13 | async-start | bytes 2228224 | tf_op jit(solution)/shard_map/reduce_scatter | solution.py:320
  1300.9 54.0 %copy-start.135 = (f32[1024]{0:T(1024)S(1)}, f32[1024]{0:T(1024)}, u32[]{:S(2)}) copy-start(f32[1024]{0:T(1024)} %get-tuple-element.3646) | copy-start | bytes 12292
  1300.9 132.6 %copy-start.128 = (f32[2,256]{1,0:T(2,128)S(1)}, f32[2,256]{1,0:T(2,128)}, u32[]{:S(2)}) copy-start(f32[2,256]{1,0:T(2,128)} %copy-done.127) | copy-start | bytes 6148
  1433.5 708.0 %copy-start.1 = (bf16[1408,1024]{1,0:T(8,128)(2,1)S(1)}, bf16[1408,1024]{1,0:T(8,128)(2,1)}, u32[]{:S(2)}) copy-start(bf16[1408,1024]{1,0:T(8,128)(2,1)} %param.52) | copy-start | bytes 8650756
  (222 other events, 817.4 us)
Sparse Core Ops, SparseCore 0:
  80.4 76.4 all-gather.8
  159.6 111.4 all-gather.10
  522.6 19.3 all-reduce.41
  559.9 22.3 all-reduce.43
  585.0 77.3 all-gather.12
  840.4 113.9 all-gather.14
  1255.0 76.8 reduce-scatter.27
  1335.0 17.6 all-reduce.45
  1355.5 82.2 reduce-scatter.19
  1440.6 77.3 reduce-scatter.17
  1520.8 122.9 reduce-scatter.21
  1646.5 126.9 reduce-scatter.23
  1776.4 126.9 reduce-scatter.25
  1906.1 78.6 reduce-scatter.13
  1987.5 74.0 reduce-scatter.11
  2064.3 77.2 reduce-scatter.15
where the time goes:
time: 2170 us; the launch traced here: 2150 us
  waiting for transfers between devices  1040 us (48%)
  matrix products  518 us (24%)
  local copies, waits for them, and re-layouts  326 us (15%)
  other arithmetic  146 us (7%)
  blocking collectives  80.2 us (4%)
    all_gather x4, waiting for transfers between devices, entering(): pieces = jax.tree.map(lambda part: lax.all_gather(part, axis), value)  265 us
    dynamic_update_slice x112, local copies, waits for them, and re-layouts, run_groups(): final_state, outputs = lax.scan(group_step, carry_state, blocks)  141 us
    reduce_scatter x1, waiting for transfers between devices, on_device(): lax.psum_scatter(grad_w_down, 'seq', scatter_dimension=1, tiled=True)  130 us
    reduce_scatter x1, waiting for transfers between devices, on_device(): lax.psum_scatter(grad_w_up, 'seq', scatter_dimension=0, tiled=True)  130 us
    reduce_scatter x1, waiting for transfers between devices, on_device(): lax.psum_scatter(grad_w_gate, 'seq', scatter_dimension=0, tiled=True)  126 us
    dot_general x120, matrix products, inverse_unit(): inverse = jnp.matmul(inverse, identity_map + power, precision=HIGHEST)  112 us
    reduce_scatter x1, waiting for transfers between devices, on_device(): lax.psum_scatter(grad_w_key, 'seq', scatter_dimension=0, tiled=True)  81.3 us
    reduce_scatter x1, waiting for transfers between devices, on_device(): lax.psum_scatter(grad_w_value, 'seq', scatter_dimension=0, tiled=True)  80 us
  transfers between devices with their start and end apart: 18, of which 14 were waited for; matrix products, arithmetic and copies ran while one was open for 17% of the time, Pallas kernels for 0%

commit v1 on v0

v1 whole, which is shorter than its diff:
```python
import functools

import jax
import jax.numpy as jnp
from jax import lax
from jax.experimental import pallas as pl
from jax.experimental.pallas import tpu as pltpu
from jax.sharding import PartitionSpec as P

DK = 128
DV = 256
CONV = 4
HALO = 16
LANES = 128
SCALE = DK ** (-0.5)
F32 = jnp.float32
BF16 = jnp.bfloat16
NN = ((1,), (0,))
NT = ((1,), (1,))
TN = ((0,), (0,))
VMEM_LIMIT = 56 * 1024 * 1024


def dot(left, right, dims=NN):
    return lax.dot_general(
        left.astype(BF16), right.astype(BF16), (dims, ((), ())), preferred_element_type=F32
    )


def halves(field):
    high = field.astype(BF16)
    return high, (field - high.astype(F32)).astype(BF16)


def dot3(left, right, dims=NN):
    left_high, left_low = halves(left)
    right_high, right_low = halves(right)
    return dot(left_high, right_high, dims) + (
        dot(left_high, right_low, dims) + dot(left_low, right_high, dims)
    )


def ones_dot(ones, field):
    high, low = halves(field)
    lowest = field - high.astype(F32) - low.astype(F32)
    return dot(ones, high) + (dot(ones, low) + dot(ones, lowest))


def rows_cols(size):
    return (
        lax.broadcasted_iota(jnp.int32, (size, size), 0),
        lax.broadcasted_iota(jnp.int32, (size, size), 1),
    )


def log1p_small(value):
    shifted = 1.0 + value
    same = shifted == 1.0
    safe = jnp.where(same, 1.0, shifted - 1.0)
    return jnp.where(same, value, jnp.log(shifted) * (value / safe))


def log_sigmoid(value):
    return jnp.minimum(value, 0.0) - log1p_small(jnp.exp(-jnp.abs(value)))


def sigmoid(value):
    return 1.0 / (1.0 + jnp.exp(-value))


def row_sum(field):
    return jnp.sum(field, axis=-1, keepdims=True)


def inverse_unit(lowers, rows, cols):
    size = lowers[0].shape[0]
    same = (rows // 16) == (cols // 16)
    eye = (rows == cols).astype(F32)
    powers = [jnp.where(same, -lower, 0.0) for lower in lowers]
    inverses = [eye + power for power in powers]
    for _ in range(3):
        powers = [dot3(power, power) for power in powers]
        inverses = [inv + dot3(inv, power) for inv, power in zip(inverses, powers)]
    block = 16
    while block * 2 <= size:
        inside = ((rows // (2 * block)) == (cols // (2 * block))) & (
            (rows // block) != (cols // block)
        )
        parts = [
            dot3(jnp.where(inside, lower, 0.0), inv) for lower, inv in zip(lowers, inverses)
        ]
        inverses = [inv - dot3(inv, part) for inv, part in zip(inverses, parts)]
        block *= 2
    return inverses


def conv_pre(extended, taps):
    total = taps[CONV - 1 : CONV] * extended
    for offset in range(CONV - 1):
        total = total + taps[offset : offset + 1] * pltpu.roll(extended, CONV - 1 - offset, 0)
    return total[HALO:]


def silu(value):
    return value * sigmoid(value)


def silu_slope(value):
    gate = sigmoid(value)
    return gate * (1.0 + value * (1.0 - gate))


def unit(field):
    inverse = lax.rsqrt(row_sum(field * field) + 1e-06)
    return field * inverse, inverse


def first_body(
    heads, x_ref, gain_ref, wq_ref, wk_ref, wv_ref, wg_ref, wgates_ref, bias_ref, cq_ref, ck_ref,
    cv_ref, mixed_ref, proj_ref, pg_ref, gates_ref, sums_ref, inv_ref, mapk_ref, fresh_ref,
    score_ref, reach_ref, local_ref, decay_ref, piece_ref, low_ref,
):
    x = x_ref[0].astype(F32)
    mixed = x * lax.rsqrt(jnp.mean(x * x, axis=-1, keepdims=True) + 1e-06) * gain_ref[...]
    mixed = mixed.astype(BF16)
    main = mixed[HALO:]
    mixed_ref[0] = main
    proj_q = dot(mixed, wq_ref[...]).astype(BF16)
    proj_k = dot(mixed, wk_ref[...]).astype(BF16)
    proj_v = dot(mixed, wv_ref[...]).astype(BF16)
    wide = heads * DK
    proj_ref[0, :, :wide] = proj_q
    proj_ref[0, :, wide : 2 * wide] = proj_k
    proj_ref[0, :, 2 * wide :] = proj_v
    pg_ref[0] = dot(main, wg_ref[...])
    gates = dot(main, wgates_ref[...]) + bias_ref[...]
    gates_ref[0] = gates
    size = main.shape[0]
    rows, cols = rows_cols(size)
    lower = rows >= cols
    strict = rows > cols
    sums = ones_dot(lower.astype(BF16), log_sigmoid(gates))
    sums_ref[0] = sums
    sums_t = jnp.transpose(sums)
    conv_q = silu(conv_pre(proj_q.astype(F32), cq_ref[...]))
    conv_k = silu(conv_pre(proj_k.astype(F32), ck_ref[...]))
    conv_v = silu(conv_pre(proj_v.astype(F32), cv_ref[...]))
    each = range(heads)
    queries = [unit(conv_q[:, h * DK : (h + 1) * DK])[0] * SCALE for h in each]
    keys = [unit(conv_k[:, h * DK : (h + 1) * DK])[0] for h in each]
    values = [conv_v[:, h * DV : (h + 1) * DV] for h in each]
    beta = [sigmoid(gates[:, h : h + 1]) for h in each]
    total = [sums[:, heads + h : heads + h + 1] for h in each]
    decay = [
        jnp.where(
            lower, jnp.exp(jnp.minimum(total[h] - sums_t[heads + h : heads + h + 1, :], 0.0)), 0.0
        )
        for h in each
    ]
    scaled = [beta[h] * keys[h] for h in each]
    lowers = [jnp.where(strict, dot3(keys[h], scaled[h], NT) * decay[h], 0.0) for h in each]
    inverses = inverse_unit(lowers, rows, cols)
    growth = [jnp.exp(total[h]) for h in each]
    last = [total[h][size - 1 : size] for h in each]
    tail = [jnp.exp(last[h] - total[h]) * scaled[h] for h in each]
    mapk = [dot3(inverses[h], growth[h] * keys[h]) for h in each]
    fresh = [dot3(inverses[h], values[h]) for h in each]
    scores = [dot3(queries[h], scaled[h], NT) * decay[h] for h in each]
    moved = [-dot3(tail[h], mapk[h], TN) for h in each]
    shift = [dot3(tail[h], fresh[h], TN) for h in each]
    reach = [growth[h] * queries[h] - dot3(scores[h], mapk[h]) for h in each]
    local = [dot3(scores[h], fresh[h]) for h in each]
    for h in each:
        piece_ref[0, h, :, :DK] = moved[h]
        piece_ref[0, h, :, DK:] = shift[h]
        low_ref[0, h, :, :DK] = moved[h].astype(BF16)
        low_ref[0, h, :, DK:] = shift[h].astype(BF16)
        inv_ref[0, h] = inverses[h]
        mapk_ref[0, h] = mapk[h]
        fresh_ref[0, h] = fresh[h]
        score_ref[0, h] = scores[h]
        reach_ref[0, h] = reach[h]
        local_ref[0, h] = local[h]
        decay_ref[0, h] = decay[h]


def join_body(pairs, level, piece_ref, got_ref, scale_ref, out_ref, low_ref):
    for p in range(pairs):
        own = piece_ref[p]
        got = got_ref[p].astype(F32)
        mine = scale_ref[level, p]
        theirs = scale_ref[level, pairs + p]
        high, low = halves(own[:, :DK])
        moved = dot(high, got_ref[p]) + dot(low, got_ref[p])
        moved = moved + mine * got
        out = jnp.concatenate([moved[:, :DK] + theirs * own[:, :DK], moved[:, DK:] + own[:, DK:]], axis=1)
        out_ref[p] = out
        low_ref[p] = out.astype(BF16)


def map_body(pairs, level, own_ref, got_ref, scale_ref, out_ref, low_ref):
    for p in range(pairs):
        own = own_ref[p]
        got = got_ref[p]
        high, low = halves(own)
        out = dot(got, high) + dot(got, low)
        out = out + scale_ref[level, pairs + p] * own + scale_ref[level, p] * got.astype(F32)
        out_ref[p] = out
        low_ref[p] = out.astype(BF16)


def entry_body(pairs, level, near_ref, far_ref, scale_ref, out_ref):
    for p in range(pairs):
        near = near_ref[p]
        far = far_ref[p]
        moved = dot(near[:, :DK], far) + scale_ref[level, p] * far.astype(F32)
        out_ref[p] = moved + near[:, DK:].astype(F32)


def back_body(pairs, level, map_ref, own_ref, got_ref, scale_ref, out_ref, low_ref):
    for p in range(pairs):
        got = got_ref[p]
        high, low = halves(map_ref[p])
        moved = dot(high, got, TN) + dot(low, got, TN)
        out = own_ref[p] + moved + scale_ref[level, p] * got.astype(F32)
        out_ref[p] = out
        low_ref[p] = out.astype(BF16)


def exit_body(pairs, level, map_ref, near_ref, far_ref, scale_ref, out_ref):
    for p in range(pairs):
        far = far_ref[p]
        moved = dot(map_ref[p], far, TN)
        out_ref[p] = near_ref[p].astype(F32) + moved + scale_ref[level, p] * far.astype(F32)


def mixer_out_body(
    heads, state_ref, fresh_ref, mapk_ref, reach_ref, local_ref, pg_ref, gain_ref, wout_ref,
    made_ref, output_ref, gated_ref, attn_ref,
):
    for h in range(heads):
        state = state_ref[0, h]
        made_ref[0, h] = fresh_ref[0, h] - dot3(mapk_ref[0, h], state)
        output = local_ref[0, h] + dot3(reach_ref[0, h], state)
        output_ref[0, :, h * DV : (h + 1) * DV] = output
        scale = lax.rsqrt(jnp.mean(output * output, axis=-1, keepdims=True) + 1e-05)
        gate = pg_ref[0, :, h * DV : (h + 1) * DV]
        gated_ref[0, :, h * DV : (h + 1) * DV] = (
            output * scale * gain_ref[...] * silu(gate)
        ).astype(BF16)
    attn_ref[0] = dot(gated_ref[0], wout_ref[...]).astype(BF16)


def feed_body(
    x_ref, mine_ref, other_ref, cot_ref, gain_ref, wgate_ref, wup_ref, wdown_ref, resid_ref,
    normed_ref, hidden_ref, dgu_ref, down_ref, dnorm_ref,
):
    units = wgate_ref.shape[1]
    attn = mine_ref[0].astype(F32) + other_ref[0].astype(F32)
    resid = x_ref[0].astype(F32) + attn
    resid_ref[0] = resid
    normed = resid * lax.rsqrt(jnp.mean(resid * resid, axis=-1, keepdims=True) + 1e-06)
    normed = (normed * gain_ref[...]).astype(BF16)
    normed_ref[0] = normed
    gate = dot(normed, wgate_ref[...])
    up = dot(normed, wup_ref[...])
    d_hidden = dot(cot_ref[0], wdown_ref[...], NT)
    sig = sigmoid(gate)
    active = gate * sig
    hidden = (active * up).astype(BF16)
    hidden_ref[0] = hidden
    d_gate = (d_hidden * up * (sig + active * (1.0 - sig))).astype(BF16)
    d_up = (d_hidden * active).astype(BF16)
    dgu_ref[0, :, :units] = d_gate
    dgu_ref[0, :, units:] = d_up
    down_ref[0] = dot(hidden, wdown_ref[...]).astype(BF16)
    dnorm_ref[0] = (dot(d_gate, wgate_ref[...], NT) + dot(d_up, wup_ref[...], NT)).astype(BF16)


def mixer_back_body(
    heads, resid_ref, mine_ref, other_ref, cot_ref, output_ref, pg_ref, reach_ref, gain_ref,
    wout_ref, ogain_ref, dresid_ref, dattn_ref, dout_ref, dpg_ref, back_ref, low_ref, dgain_ref,
    dogain_ref,
):
    step = pl.program_id(0)
    resid = resid_ref[0]
    inverse = lax.rsqrt(jnp.mean(resid * resid, axis=-1, keepdims=True) + 1e-06)
    unit_resid = resid * inverse
    d_normed = mine_ref[0].astype(F32) + other_ref[0].astype(F32)
    d_gain = jnp.sum(d_normed * unit_resid, axis=0, keepdims=True)
    d_unit = d_normed * gain_ref[...]
    d_resid = inverse * (
        d_unit - unit_resid * jnp.mean(d_unit * unit_resid, axis=-1, keepdims=True)
    )
    d_resid = d_resid + cot_ref[0].astype(F32)
    dresid_ref[0] = d_resid
    d_attn = d_resid.astype(BF16)
    dattn_ref[0] = d_attn
    d_gated = dot(d_attn, wout_ref[...], NT)
    d_ogain = jnp.zeros((1, DV), F32)
    for h in range(heads):
        part = slice(h * DV, (h + 1) * DV)
        output = output_ref[0, :, part]
        inverse = lax.rsqrt(jnp.mean(output * output, axis=-1, keepdims=True) + 1e-05)
        unit_out = output * inverse
        gate = pg_ref[0, :, part]
        grad = d_gated[:, part]
        active = silu(gate)
        d_ogain = d_ogain + jnp.sum(grad * unit_out * active, axis=0, keepdims=True)
        dpg_ref[0, :, part] = (grad * unit_out * ogain_ref[...] * silu_slope(gate)).astype(BF16)
        d_unit = grad * ogain_ref[...] * active
        d_out = inverse * (d_unit - unit_out * jnp.mean(d_unit * unit_out, axis=-1, keepdims=True))
        dout_ref[0, :, part] = d_out
        back = dot3(reach_ref[0, h], d_out, TN)
        back_ref[0, h] = back
        low_ref[0, h] = back.astype(BF16)

    @pl.when(step == 0)
    def _():
        dgain_ref[...] = d_gain
        dogain_ref[...] = d_ogain

    @pl.when(step > 0)
    def _():
        dgain_ref[...] += d_gain
        dogain_ref[...] += d_ogain


def conv_back(grad, extended, taps, pre):
    d_pre = grad * silu_slope(pre)
    padded = jnp.concatenate([jnp.zeros((HALO, d_pre.shape[1]), F32), d_pre], axis=0)
    length = padded.shape[0]
    d_ext = taps[CONV - 1 : CONV] * padded
    d_taps = []
    for offset in range(CONV):
        back = CONV - 1 - offset
        if back:
            d_ext = d_ext + taps[offset : offset + 1] * pltpu.roll(padded, length - back, 0)
            shifted = pltpu.roll(extended, back, 0)
        else:
            shifted = extended
        d_taps.append(jnp.sum(padded * shifted, axis=0, keepdims=True))
    return d_ext, jnp.concatenate(d_taps, axis=0)


def early_body(
    heads, proj_ref, gates_ref, sums_ref, dout_ref, state_ref, made_ref, inv_ref, score_ref,
    decay_ref, cq_ref, ck_ref, xone_ref, xmap_ref, dkey_ref, dcol_ref, dext_ref, dtap_ref,
):
    step = pl.program_id(0)
    wide = heads * DK
    ext_q = proj_ref[0, :, :wide].astype(F32)
    ext_k = proj_ref[0, :, wide : 2 * wide].astype(F32)
    pre_q = conv_pre(ext_q, cq_ref[...])
    conv_q = silu(pre_q)
    conv_k = silu(conv_pre(ext_k, ck_ref[...]))
    gates = gates_ref[0]
    sums = sums_ref[0]
    size = gates.shape[0]
    each = range(heads)
    units = [unit(conv_q[:, h * DK : (h + 1) * DK]) for h in each]
    queries = [units[h][0] * SCALE for h in each]
    keys = [unit(conv_k[:, h * DK : (h + 1) * DK])[0] for h in each]
    beta = [sigmoid(gates[:, h : h + 1]) for h in each]
    total = [sums[:, heads + h : heads + h + 1] for h in each]
    growth = [jnp.exp(total[h]) for h in each]
    tail = [jnp.exp(total[h][size - 1 : size] - total[h]) * beta[h] * keys[h] for h in each]
    d_out = [dout_ref[0, :, h * DV : (h + 1) * DV] for h in each]
    d_made = [dot3(score_ref[0, h], d_out[h], TN) for h in each]
    d_score = [dot3(d_out[h], made_ref[0, h], NT) * decay_ref[0, h] for h in each]
    d_query = [
        dot3(d_score[h], beta[h] * keys[h]) + dot3(growth[h] * d_out[h], state_ref[0, h], NT)
        for h in each
    ]
    d_key = [dot3(d_score[h], queries[h], TN) for h in each]
    x_one = [dot3(inv_ref[0, h], d_made[h], TN) for h in each]
    x_map = [dot3(inv_ref[0, h], tail[h], TN) for h in each]
    lanes = lax.broadcasted_iota(jnp.int32, (size, LANES), 1)
    cols = jnp.zeros((size, LANES), F32)
    grads = []
    for h in each:
        xone_ref[0, h] = x_one[h]
        xmap_ref[0, h] = x_map[h]
        dkey_ref[0, h] = beta[h] * d_key[h]
        key_sum = row_sum(d_key[h] * keys[h])
        cols = cols + jnp.where(lanes == h, key_sum, 0.0)
        d_total = row_sum(d_query[h] * queries[h]) - beta[h] * key_sum
        cols = cols + jnp.where(lanes == heads + h, d_total, 0.0)
        unit_q, inverse = units[h]
        d_unit = d_query[h] * SCALE
        grads.append(inverse * (d_unit - unit_q * row_sum(d_unit * unit_q)))
    dcol_ref[0] = cols
    d_ext, d_taps = conv_back(jnp.concatenate(grads, axis=1), ext_q, cq_ref[...], pre_q)
    dext_ref[0] = d_ext

    @pl.when(step == 0)
    def _():
        dtap_ref[...] = d_taps

    @pl.when(step > 0)
    def _():
        dtap_ref[...] += d_taps


def late_body(
    heads, proj_ref, gates_ref, sums_ref, dend_ref, state_ref, made_ref, decay_ref, xone_ref,
    xmap_ref, dkey_ref, dcol_ref, dextq_ref, ck_ref, cv_ref, dext_ref, dgates_ref, dtap_ref, dbias_ref,
):
    step = pl.program_id(0)
    wide = heads * DK
    ext_k = proj_ref[0, :, wide : 2 * wide].astype(F32)
    ext_v = proj_ref[0, :, 2 * wide :].astype(F32)
    pre_k = conv_pre(ext_k, ck_ref[...])
    pre_v = conv_pre(ext_v, cv_ref[...])
    conv_k = silu(pre_k)
    gates = gates_ref[0]
    sums = sums_ref[0]
    size = gates.shape[0]
    rows, cols = rows_cols(size)
    strict = rows > cols
    each = range(heads)
    units = [unit(conv_k[:, h * DK : (h + 1) * DK]) for h in each]
    keys = [units[h][0] for h in each]
    beta = [sigmoid(gates[:, h : h + 1]) for h in each]
    total = [sums[:, heads + h : heads + h + 1] for h in each]
    growth = [jnp.exp(total[h]) for h in each]
    left = [jnp.exp(total[h][size - 1 : size] - total[h]) for h in each]
    d_end = [dend_ref[0, h] for h in each]
    made = [made_ref[0, h] for h in each]
    state = [state_ref[0, h] for h in each]
    d_rhs = [xone_ref[0, h] + dot3(xmap_ref[0, h], d_end[h]) for h in each]
    d_tail = [dot3(made[h], d_end[h], NT) for h in each]
    d_lower = [
        jnp.where(strict, -dot3(d_rhs[h], made[h], NT) * decay_ref[0, h], 0.0) for h in each
    ]
    d_plain = [
        dot3(d_lower[h], beta[h] * keys[h]) - dot3(growth[h] * d_rhs[h], state[h], NT) for h in each
    ]
    d_turned = [dot3(d_lower[h], keys[h], TN) for h in each]
    lanes = lax.broadcasted_iota(jnp.int32, (size, LANES), 1)
    places = lax.broadcasted_iota(jnp.int32, (size, 1), 0)
    d_col = dcol_ref[0]
    grads_k = []
    for h in each:
        turned = row_sum(d_turned[h] * keys[h])
        tails = row_sum(d_tail[h] * keys[h])
        tail_weight = left[h] * beta[h]
        d_key = d_plain[h] + beta[h] * d_turned[h] + tail_weight * d_tail[h] + dkey_ref[0, h]
        d_total = row_sum(d_plain[h] * keys[h]) - beta[h] * turned - tail_weight * tails
        ended = jnp.sum(tail_weight * tails, axis=0, keepdims=True)
        whole = jnp.sum(row_sum(d_end[h] * state[h]), axis=0, keepdims=True)
        ended = ended + growth[h][size - 1 : size] * whole
        d_total = d_total + jnp.where(places == size - 1, ended, 0.0)
        d_col = d_col + jnp.where(lanes == h, turned + left[h] * tails, 0.0)
        d_col = d_col + jnp.where(lanes == heads + h, d_total, 0.0)
        unit_k, inverse = units[h]
        grads_k.append(inverse * (d_key - unit_k * row_sum(d_key * unit_k)))
    upper = (rows <= cols).astype(BF16)
    d_decay = ones_dot(upper, d_col)
    rate = sigmoid(gates)
    d_gates = jnp.where(
        lanes < heads, d_col * rate * (1.0 - rate), d_decay / (1.0 + jnp.exp(gates))
    )
    d_gates = jnp.where(lanes < 2 * heads, d_gates, 0.0)
    dgates_ref[0] = d_gates.astype(BF16)
    d_bias = jnp.sum(d_gates, axis=0, keepdims=True)
    dext_k, dtaps_k = conv_back(jnp.concatenate(grads_k, axis=1), ext_k, ck_ref[...], pre_k)
    dext_v, dtaps_v = conv_back(jnp.concatenate(d_rhs, axis=1), ext_v, cv_ref[...], pre_v)
    dext_ref[0, :, :wide] = dextq_ref[0]
    dext_ref[0, :, wide : 2 * wide] = dext_k
    dext_ref[0, :, 2 * wide :] = dext_v

    @pl.when(step == 0)
    def _():
        dtap_ref[:, :wide] = dtaps_k
        dtap_ref[:, wide:] = dtaps_v
        dbias_ref[...] = d_bias

    @pl.when(step > 0)
    def _():
        dtap_ref[:, :wide] += dtaps_k
        dtap_ref[:, wide:] += dtaps_v
        dbias_ref[...] += d_bias


def input_back_body(
    dext_ref, edge_ref, dpg_ref, dgates_ref, wq_ref, wk_ref, wv_ref, wg_ref, wgates_ref, dproj_ref,
    dmixed_ref,
):
    wide = wq_ref.shape[1]
    own = dext_ref[0, HALO:]
    size = own.shape[0]
    d_proj = jnp.concatenate([own[: size - HALO], own[size - HALO :] + edge_ref[0]], axis=0)
    d_proj = d_proj.astype(BF16)
    dproj_ref[0] = d_proj
    d_mixed = dot(d_proj[:, :wide], wq_ref[...], NT)
    d_mixed = d_mixed + dot(d_proj[:, wide : 2 * wide], wk_ref[...], NT)
    d_mixed = d_mixed + dot(d_proj[:, 2 * wide :], wv_ref[...], NT)
    d_mixed = d_mixed + dot(dpg_ref[0], wg_ref[...], NT)
    d_mixed = d_mixed + dot(dgates_ref[0], wgates_ref[...], NT)
    dmixed_ref[0] = d_mixed.astype(BF16)


def last_body(x_ref, mine_ref, other_ref, dresid_ref, gain_ref, grad_ref, dgain_ref):
    step = pl.program_id(0)
    x = x_ref[0].astype(F32)
    inverse = lax.rsqrt(jnp.mean(x * x, axis=-1, keepdims=True) + 1e-06)
    unit_x = x * inverse
    d_mixed = mine_ref[0].astype(F32) + other_ref[0].astype(F32)
    d_gain = jnp.sum(d_mixed * unit_x, axis=0, keepdims=True)
    d_unit = d_mixed * gain_ref[...]
    back = inverse * (d_unit - unit_x * jnp.mean(d_unit * unit_x, axis=-1, keepdims=True))
    grad_ref[0] = dresid_ref[0] + back

    @pl.when(step == 0)
    def _():
        dgain_ref[...] = d_gain

    @pl.when(step > 0)
    def _():
        dgain_ref[...] += d_gain


def by_seq(shape):
    rest = len(shape) - 1
    return pl.BlockSpec((1,) + tuple(shape[1:]), lambda s: (s,) + (0,) * rest)


def whole(shape):
    rest = len(shape)
    return pl.BlockSpec(tuple(shape), lambda s: (0,) * rest)


def call(body, name, seqs, parts, shared, outs, sums=(), flops=0):
    operands = list(parts) + list(shared)
    out_shape = [jax.ShapeDtypeStruct(shape, kind) for shape, kind in list(outs) + list(sums)]
    moved = sum(a.size * a.dtype.itemsize for a in operands)
    moved += sum(a.size * a.dtype.itemsize for a in out_shape)
    return pl.pallas_call(
        body,
        grid=(seqs,),
        in_specs=[by_seq(a.shape) for a in parts] + [whole(a.shape) for a in shared],
        out_specs=[by_seq(shape) for shape, _ in outs] + [whole(shape) for shape, _ in sums],
        out_shape=out_shape,
        compiler_params=pltpu.CompilerParams(vmem_limit_bytes=VMEM_LIMIT),
        cost_estimate=pl.CostEstimate(flops=int(flops), bytes_accessed=int(moved), transcendentals=0),
        name=name,
    )(*operands)


def small_call(body, name, arrays, scales, outs):
    operands = list(arrays) + [scales]
    out_shape = [jax.ShapeDtypeStruct(shape, kind) for shape, kind in outs]
    moved = sum(a.size * a.dtype.itemsize for a in list(arrays) + out_shape)
    return pl.pallas_call(
        body,
        in_specs=[pl.BlockSpec(memory_space=pltpu.VMEM)] * len(arrays)
        + [pl.BlockSpec(memory_space=pltpu.SMEM)],
        out_specs=[pl.BlockSpec(memory_space=pltpu.VMEM)] * len(outs),
        out_shape=out_shape,
        compiler_params=pltpu.CompilerParams(vmem_limit_bytes=VMEM_LIMIT),
        cost_estimate=pl.CostEstimate(flops=200_000_000, bytes_accessed=int(moved), transcendentals=0),
        name=name,
    )(*operands)


def passed_along(block, axis, distance):
    devices = range(lax.axis_size(axis))
    route = [(i - distance, i) for i in devices if i - distance in devices]
    return lax.ppermute(block, axis, route)


def swapped(block):
    count = lax.axis_size("head")
    return lax.ppermute(block, "head", [(i, i ^ 1) for i in range(count)])


def on_device(
    tokens, w_query, w_key, w_value, w_outgate, w_gates, gate_bias, conv_query, conv_key,
    conv_value, out_gain, w_out, mix_gain, ffn_gain, w_gate, w_up, w_down, cotangent,
):
    seqs, size, width = tokens.shape
    heads = gate_bias.shape[1]
    pairs = seqs * heads
    units = w_gate.shape[1]
    count, me = lax.axis_size("seq"), lax.axis_index("seq")
    wide = heads * DK
    out_wide = heads * DV
    proj_wide = 2 * wide + out_wide

    halo = passed_along(tokens[:, size - HALO :], "seq", 1)
    x_ext = jnp.concatenate([halo, tokens], axis=1)
    gates_w = jnp.swapaxes(w_gates, 0, 1).reshape(width, 2 * heads)
    gates_w = jnp.pad(gates_w, ((0, 0), (0, LANES - 2 * heads)))
    bias = jnp.pad(gate_bias.reshape(1, 2 * heads), ((0, 0), (0, LANES - 2 * heads)))
    mix_row = mix_gain.reshape(1, width)
    ffn_row = ffn_gain.reshape(1, width)
    out_row = out_gain.reshape(1, DV)
    square = (seqs, heads, size, size)
    by_key = (seqs, heads, size, DK)
    by_value = (seqs, heads, size, DV)
    (
        mixed, proj, proj_g, gates, sums, inv, mapk, fresh, score, reach, local, decay, piece, low,
    ) = call(
        functools.partial(first_body, heads), "project_and_local", seqs, [x_ext],
        [mix_row, w_query, w_key, w_value, w_outgate, gates_w, bias, conv_query, conv_key, conv_value],
        [
            ((seqs, size, width), BF16), ((seqs, size + HALO, proj_wide), BF16),
            ((seqs, size, out_wide), F32), ((seqs, size, LANES), F32), ((seqs, size, LANES), F32),
            (square, F32), (by_key, F32), (by_value, F32), (square, F32), (by_key, F32),
            (by_value, F32), (square, F32), ((seqs, heads, DK, DK + DV), F32),
            ((seqs, heads, DK, DK + DV), BF16),
        ],
        flops=1e10,
    )

    ended = sums[:, size - 1, heads : 2 * heads].reshape(pairs)
    all_ended = lax.all_gather(ended, "seq")
    spans = []
    dists = []
    reach_by = 1
    while reach_by * 2 < count:
        dists.append(reach_by)
        reach_by *= 2
    for d in dists:
        spans.append(((me - d + 1, me), (me - 2 * d + 1, me - d)))
    spans.append(((me - reach_by, me - 1), (me, me - 1)))
    for d in dists:
        spans.append(((me, me + d - 1), (me + d, me + 2 * d - 1)))
    spans.append(((me + 1, me + reach_by), (me, me - 1)))
    low_end = jnp.stack([jnp.stack([a[0] for a in pair]) for pair in spans])[..., None]
    high_end = jnp.stack([jnp.stack([a[1] for a in pair]) for pair in spans])[..., None]
    index = jnp.arange(count)
    within = ((index >= low_end) & (index <= high_end)).astype(F32)
    scales = jnp.exp(jnp.sum(within[..., None] * all_ended, axis=2)).reshape(len(spans), 2 * pairs)

    piece = piece.reshape(pairs, DK, DK + DV)
    low = low.reshape(pairs, DK, DK + DV)
    back_maps = [piece[:, :, :DK]]
    back_low = low[:, :, :DK]
    joined, state_shape = (piece, (pairs, DK, DV))
    for level, d in enumerate(dists):
        got = passed_along(low, "seq", d)
        joined, low = small_call(
            functools.partial(join_body, pairs, level), "join", [joined, got], scales,
            [(piece.shape, F32), (piece.shape, BF16)],
        )
    near = passed_along(low, "seq", 1)
    far = passed_along(low[:, :, DK:], "seq", 1 + reach_by)
    (state,) = small_call(
        functools.partial(entry_body, pairs, len(dists)), "entry", [near, far], scales,
        [(state_shape, F32)],
    )
    state = state.reshape(seqs, heads, DK, DV)

    made, output, gated, attn = call(
        functools.partial(mixer_out_body, heads), "mixer_out", seqs,
        [state, fresh, mapk, reach, local, proj_g], [out_row, w_out],
        [
            (by_value, F32), ((seqs, size, out_wide), F32), ((seqs, size, out_wide), BF16),
            ((seqs, size, width), BF16),
        ],
        flops=1.5e9,
    )
    attn_other = swapped(attn)

    resid, normed, hidden, d_gu, down, d_norm = call(
        feed_body, "feed_forward", seqs, [tokens, attn, attn_other, cotangent],
        [ffn_row, w_gate, w_up, w_down],
        [
            ((seqs, size, width), F32), ((seqs, size, width), BF16), ((seqs, size, units), BF16),
            ((seqs, size, 2 * units), BF16), ((seqs, size, width), BF16),
            ((seqs, size, width), BF16),
        ],
        flops=1.2e10,
    )
    d_norm_other = swapped(d_norm)
    down_other = swapped(down)

    level0 = len(dists) + 1
    for level, d in enumerate(dists):
        got = passed_along(back_low, "seq", -d)
        new_map, back_low = small_call(
            functools.partial(map_body, pairs, level0 + level), "join_maps", [back_maps[-1], got],
            scales, [((pairs, DK, DK), F32), ((pairs, DK, DK), BF16)],
        )
        back_maps.append(new_map)
    near_map = passed_along(back_low, "seq", -1)

    d_resid, d_attn, d_out, d_pg, back, low, d_ffn_gain, d_out_gain = call(
        functools.partial(mixer_back_body, heads), "mixer_back", seqs,
        [resid, d_norm, d_norm_other, cotangent, output, proj_g, reach],
        [ffn_row, w_out, out_row],
        [
            ((seqs, size, width), F32), ((seqs, size, width), BF16), ((seqs, size, out_wide), F32),
            ((seqs, size, out_wide), BF16), ((seqs, heads, DK, DV), F32),
            ((seqs, heads, DK, DV), BF16),
        ],
        [((1, width), F32), ((1, DV), F32)],
        flops=1.5e9,
    )

    back = back.reshape(state_shape)
    low = low.reshape(state_shape)
    for level, d in enumerate(dists):
        got = passed_along(low, "seq", -d)
        back, low = small_call(
            functools.partial(back_body, pairs, level0 + level), "join_back",
            [back_maps[level], back, got], scales, [(state_shape, F32), (state_shape, BF16)],
        )
    near = passed_along(low, "seq", -1)
    far = passed_along(low, "seq", -1 - reach_by)
    (d_end,) = small_call(
        functools.partial(exit_body, pairs, level0 + len(dists)), "exit", [near_map, near, far],
        scales, [(state_shape, F32)],
    )
    d_end = d_end.reshape(seqs, heads, DK, DV)

    x_one, x_map, d_key, d_col, dext_q, dtap_q = call(
        functools.partial(early_body, heads), "delta_back_early", seqs,
        [proj, gates, sums, d_out, state, made, inv, score, decay], [conv_query, conv_key],
        [
            (by_value, F32), (by_key, F32), (by_key, F32), ((seqs, size, LANES), F32),
            ((seqs, size + HALO, wide), F32),
        ],
        [((CONV, wide), F32)],
        flops=3e9,
    )
    d_ext, d_gates, dtap_kv, d_bias = call(
        functools.partial(late_body, heads), "delta_back_late", seqs,
        [
            proj, gates, sums, d_end, state, made, decay, x_one, x_map, d_key, d_col, dext_q,
        ],
        [conv_key, conv_value],
        [((seqs, size + HALO, proj_wide), F32), ((seqs, size, LANES), BF16)],
        [((CONV, wide + out_wide), F32), ((1, LANES), F32)],
        flops=3e9,
    )
    edges = passed_along(d_ext[:, :HALO], "seq", -1)
    d_proj, d_mixed = call(
        input_back_body, "input_back", seqs, [d_ext, edges, d_pg, d_gates],
        [w_query, w_key, w_value, w_outgate, gates_w],
        [((seqs, size, proj_wide), BF16), ((seqs, size, width), BF16)],
        flops=1.7e9,
    )
    d_mixed_other = swapped(d_mixed)
    grad_input, d_mix_gain = call(
        last_body, "first_norm_back", seqs, [tokens, d_mixed, d_mixed_other, d_resid], [mix_row],
        [((seqs, size, width), F32)], [((1, width), F32)],
    )
    result = (resid + (down.astype(F32) + down_other.astype(F32))).astype(BF16)

    def weight_grad(left, right):
        return jnp.einsum("spa,spb->ab", left, right, preferred_element_type=F32).astype(BF16)

    def scattered(grad):
        return lax.psum_scatter(grad, "seq", scatter_dimension=0, tiled=True).astype(F32)

    gate_up = scattered(weight_grad(normed, d_gu))
    down_t = scattered(weight_grad(cotangent, hidden))
    out_t = scattered(weight_grad(d_attn, gated))
    right = jnp.concatenate([d_proj, d_pg, d_gates], axis=2)
    ins = scattered(weight_grad(mixed, right))

    out_gain_sum = d_out_gain + swapped(d_out_gain)
    small = jnp.concatenate(
        [
            dtap_q.reshape(-1), dtap_kv.reshape(-1), d_bias.reshape(-1), out_gain_sum.reshape(-1),
            d_mix_gain.reshape(-1), d_ffn_gain.reshape(-1),
        ]
    )
    small = lax.psum(small, "seq")
    cuts = [0]
    for length in (CONV * wide, CONV * (wide + out_wide), LANES, DV, width, width):
        cuts.append(cuts[-1] + length)
    pieces = [small[a:b] for a, b in zip(cuts[:-1], cuts[1:])]
    taps_kv = pieces[1].reshape(CONV, wide + out_wide)
    share = width // count
    g0 = proj_wide + out_wide
    grad_gates = jnp.swapaxes(ins[:, g0 : g0 + 2 * heads].reshape(share, 2, heads), 0, 1)
    return (
        result,
        grad_input,
        ins[:, :wide],
        ins[:, wide : 2 * wide],
        ins[:, 2 * wide : proj_wide],
        ins[:, proj_wide : proj_wide + out_wide],
        grad_gates,
        pieces[2][: 2 * heads].reshape(2, heads),
        pieces[0].reshape(CONV, wide),
        taps_kv[:, :wide],
        taps_kv[:, wide:],
        pieces[3],
        jnp.swapaxes(out_t, 0, 1),
        lax.dynamic_slice_in_dim(pieces[4], me * share, share),
        lax.dynamic_slice_in_dim(pieces[5], me * share, share),
        gate_up[:, :units],
        gate_up[:, units:],
        jnp.swapaxes(down_t, 0, 1),
    )


def solution(mesh):
    return jax.shard_map(
        on_device,
        mesh=mesh,
        in_specs=(
            P(None, "seq", None),
            P(None, "head"),
            P(None, "head"),
            P(None, "head"),
            P(None, "head"),
            P(None, None, "head"),
            P(None, "head"),
            P(None, "head"),
            P(None, "head"),
            P(None, "head"),
            P(),
            P("head", None),
            P(),
            P(),
            P(None, "head"),
            P(None, "head"),
            P("head", None),
            P(None, "seq", None),
        ),
        out_specs=(
            P(None, "seq", None),
            P(None, "seq", None),
            P("seq", "head"),
            P("seq", "head"),
            P("seq", "head"),
            P("seq", "head"),
            P(None, "seq", "head"),
            P(None, "head"),
            P(None, "head"),
            P(None, "head"),
            P(None, "head"),
            P(),
            P("head", "seq"),
            P("seq"),
            P("seq"),
            P("seq", "head"),
            P("seq", "head"),
            P("head", "seq"),
        ),
        check_vma=False,
    )
```

time: 2170 us -> 558 us (0.26)
  waiting for transfers between devices: 1040 us -> 223 us
  matrix products: 518 us -> 17.9 us
  local copies, waits for them, and re-layouts: 326 us -> 41.1 us
  other arithmetic: 146 us -> 7.33 us
  Pallas kernels: 0 us -> 102 us
  blocking collectives: 80.2 us -> 117 us
    reduce_scatter x8 -> x3, waiting for transfers between devices: 703 us -> 147 us  [scattered(): lax.psum_scatter(grad, 'seq', scatter_dimension=0, tiled=True).astype(F32)]
    dot_general x453 -> x4, matrix products: 518 us -> 17.9 us  [weight_grad(): jnp.einsum('spa,spb->ab', left, right, preferred_element_type=F32)]
    all_gather x4 -> x0, waiting for transfers between devices: 265 us -> none  [entering(): pieces = jax.tree.map(lambda part: lax.all_gather(part, axis), value)]
    dynamic_update_slice x112 -> x0, local copies, waits for them, and re-layouts: 141 us -> none  [run_groups(): final_state, outputs = lax.scan(group_step, carry_state, blocks)]
    pallas_call x0 -> x19, Pallas kernels: none -> 102 us  [the longest x8 77 us: call(): pl.pallas_call(body, grid=(seqs,), in_specs=[by_seq(a.shape) for a in par...]
    ppermute x2 -> x16, waiting for transfers between devices: 0.01 us -> 68.1 us  [passed_along(): return lax.ppermute(block, axis, route)]
    reduce_sum x51 -> x1, other arithmetic: 58.4 us -> 0.09 us  [on_device(): jnp.sum(within[..., None] * all_ended, axis=2)]
    psum x3 -> x0, waiting for transfers between devices: 42.8 us -> none  [the longest x1 19.2 us: on_device(): lax.psum(product(hidden, w_down).astype(jnp.bfloat16), 'head')]
  transfers between devices with their start and end apart: 18 -> 25, of which waited for: 14 -> 15; matrix products, arithmetic and copies ran while one was open for 17% -> 8% of each run, Pallas kernels for 0% -> 8%
where the time goes in v1:
time: 558 us; the launch traced here: 557 us
  waiting for transfers between devices  223 us (40%)
  blocking collectives  117 us (21%)
  Pallas kernels  102 us (18%)
  local copies, waits for them, and re-layouts  41.1 us (7%)
  starting transfers between devices  34 us (6%)
  matrix products  17.9 us (3%)
  between operations  14.2 us (3%)
  other arithmetic  7.33 us (1%)
    reduce_scatter x3, waiting for transfers between devices, scattered(): lax.psum_scatter(grad, 'seq', scatter_dimension=0, tiled=True).astype(F32)  147 us
    pallas_call x8, Pallas kernels, call(): pl.pallas_call(body, grid=(seqs,), in_specs=[by_seq(a.shape) for a in par...  77 us
    psum x1, blocking collectives, on_device(): small = lax.psum(small, 'seq')  76.4 us
    ppermute x16, waiting for transfers between devices, passed_along(): return lax.ppermute(block, axis, route)  68.1 us
    all_gather x1, blocking collectives, on_device(): all_ended = lax.all_gather(ended, 'seq')  40.1 us
    ppermute x16, starting transfers between devices, passed_along(): return lax.ppermute(block, axis, route)  32.7 us
    pallas_call x11, Pallas kernels, small_call(): pl.pallas_call(body, in_specs=[pl.BlockSpec(memory_space=pltpu.VMEM)] * l...  25.3 us
    unnamed x70, local copies, waits for them, and re-layouts  20.5 us
  transfers between devices with their start and end apart: 25, of which 15 were waited for; matrix products, arithmetic and copies ran while one was open for 8% of the time, Pallas kernels for 8%

profile of v1, /device:TPU:0, one launch (start us, length us, event | category | flops | bytes accessed | tf_op | source)
XLA Modules:
  0.0 556.8 jit_solution(9391911411722576570)
XLA Ops:
  8.1 4.8 collective-permute-start
  16.7 2.3 pad_maximum_fusion.x_ref
  19.0 19.2 %project_and_local.1 = (bf16[2,256,1024]{2,1,0:T(8,128)(2,1)}, bf16[2,272,1024]{2,1,0:T(8,128)(2,1)}, f32[2,256,512]{2,1,0:T(8,128)}, f32[2,256,128]{2,1,0:T(8,1...) custom-call(bf16[2,272,1024]{2,1,0:T(8,128)(2,1)} %pad_maximum_fusio, ...), custom_call_target="tpu_custom_call" | custom-call | flops 10000000000 | bytes 15749632 | tf_op jit(solution)/shard_map/project_and_local/pallas_call | solution.py:539
  38.2 3.4 collective-permute-start.1
  42.6 40.1 %all-gather = f32[16,1,4]{2,1,0:T(1,128)S(1)} all-gather(f32[1,1,4]{2,1,0:T(1,128)S(1)} %reshape.142), channel_id=1, replica_groups=mesh['seq'=16,'head'=2] {'seq'}, dimensions={0}, use_global_device_ids=true | all-gather | bytes 272 | tf_op jit(solution)/shard_map/all_gather | solution.py:618
  84.3 2.6 join.3
  87.0 1.3 collective-permute-start.2
  88.3 5.6 %collective-permute-done.2.got_ref = bf16[4,128,384]{2,1,0:T(8,128)(2,1)S(1)} collective-permute-done((bf16[4,128,384]{2,1,0:T(8,128)(2,1)}, bf16[4,128,384]{2,1,0:T(8,128)(2,1)S(1)}, u32[]{:S(2)}, u32[]{:S(2)}) %collective-permute-start.2) | collective-permute-done | bytes 393248 | tf_op jit(solution)/shard_map/ppermute | solution.py:570
  94.6 2.7 join.4
  97.3 2.2 collective-permute-start.3
  99.5 5.6 %collective-permute-done.3.got_ref = bf16[4,128,384]{2,1,0:T(8,128)(2,1)S(1)} collective-permute-done((bf16[4,128,384]{2,1,0:T(8,128)(2,1)}, bf16[4,128,384]{2,1,0:T(8,128)(2,1)S(1)}, u32[]{:S(2)}, u32[]{:S(2)}) %collective-permute-start.3) | collective-permute-done | bytes 393248 | tf_op jit(solution)/shard_map/ppermute | solution.py:570
  105.8 2.6 join.5
  108.5 1.3 collective-permute-start.4
  110.8 6.6 %collective-permute-start.5 = (bf16[4,128,256]{2,1,0:T(8,128)(2,1)S(1)}, bf16[4,128,256]{2,1,0:T(8,128)(2,1)S(1)}, u32[]{:S(2)}, u32[]{:S(2)}) collective-permute-start(bf16[4,128,256]{2,1,0:T(8,128)(2,1)S(1)} %slice.75), channel_id=1, source_target_pairs={{0,18},{2,20},{4,22},{6,24},{8,26},{10,28},{12,30},{1,19},{3,21},{... | collective-permute-start | bytes 786440 | tf_op jit(solution)/shard_map/ppermute | solution.py:570
  117.3 3.7 collective-permute-done.5.far_ref
  122.5 2.1 entry.1
  124.6 5.1 mixer_out.1
  129.8 2.9 collective-permute-done.6.other_ref
  133.6 16.3 %feed_forward.1 = (f32[2,256,1024]{2,1,0:T(8,128)}, bf16[2,256,1024]{2,1,0:T(8,128)(2,1)}, bf16[2,256,1408]{2,1,0:T(8,128)(2,1)}, bf16[2,256,2816]{2,1,0:T(8,128...) custom-call(bf16[2,256,1024]{2,1,0:T(8,128)(2,1)} %x_ref.3, ...), custom_call_target="tpu_custom_call" | custom-call | flops 12000000000 | bytes 22417408 | tf_op jit(solution)/shard_map/feed_forward/pallas_call | solution.py:539
  150.1 2.7 collective-permute-done.12.other_ref
  153.8 7.5 %mixer_back.1 = (f32[2,256,1024]{2,1,0:T(8,128)}, bf16[2,256,1024]{2,1,0:T(8,128)(2,1)}, f32[2,256,512]{2,1,0:T(8,128)}, bf16[2,256,512]{2,1,0:T(8,128)(2,1)}, f...) custom-call(f32[2,256,1024]{2,1,0:T(8,128)} %get-tuple-element.93.resid_ref,, ...), custom_call_target="tpu_custom_call" | custom-call | flops 1500000000 | bytes 14428160 | tf_op jit(solution)/shard_map/mixer_back/pallas_call | solution.py:539
  161.4 3.0 bitcast_convert_fusion.3
  164.4 3.3 fusion
  167.8 2.9 copy.139
  171.6 1.3 collective-permute-start.13
  172.9 1.7 slice.94.own_ref.map_ref
  174.6 11.2 %collective-permute-done.13.got_ref = bf16[4,128,256]{2,1,0:T(8,128)(2,1)S(1)} collective-permute-done((bf16[4,128,256]{2,1,0:T(8,128)(2,1)S(1)}, bf16[4,128,256]{2,1,0:T(8,128)(2,1)S(1)}, u32[]{:S(2)}, u32[]{:S(2)}) %collective-permute-start.13) | collective-permute-done | bytes 262176 | tf_op jit(solution)/shard_map/ppermute | solution.py:570
  186.5 2.4 join_back.3
  188.9 1.3 collective-permute-start.14
  191.1 1.3 collective-permute-start.8
  192.4 9.5 %collective-permute-done.8.got_ref = bf16[4,128,128]{2,1,0:T(8,128)(2,1)S(1)} collective-permute-done((bf16[4,128,128]{2,1,0:T(8,128)(2,1)S(1)}, bf16[4,128,128]{2,1,0:T(8,128)(2,1)S(1)}, u32[]{:S(2)}, u32[]{:S(2)}) %collective-permute-start.8) | collective-permute-done | bytes 131104 | tf_op jit(solution)/shard_map/ppermute | solution.py:570
  202.6 2.0 join_maps.3
  204.6 1.3 collective-permute-start.9
  206.6 2.4 join_back.4
  209.0 1.3 collective-permute-start.15
  210.3 2.2 collective-permute-done.9.got_ref
  213.1 2.0 join_maps.4
  215.1 1.3 collective-permute-start.10
  216.4 8.8 %collective-permute-done.10.got_ref = bf16[4,128,128]{2,1,0:T(8,128)(2,1)S(1)} collective-permute-done((bf16[4,128,128]{2,1,0:T(8,128)(2,1)}, bf16[4,128,128]{2,1,0:T(8,128)(2,1)S(1)}, u32[]{:S(2)}, u32[]{:S(2)}) %collective-permute-start.10) | collective-permute-done | bytes 131104 | tf_op jit(solution)/shard_map/ppermute | solution.py:570
  225.9 2.0 join_maps.5
  227.8 1.3 collective-permute-start.11
  229.8 2.4 join_back.5
  232.2 1.3 collective-permute-start.16
  233.5 1.5 collective-permute-start.17
  235.0 8.2 %delta_back_early.1 = (f32[2,2,256,256]{3,2,1,0:T(8,128)}, f32[2,2,256,128]{3,2,1,0:T(8,128)}, f32[2,2,256,128]{3,2,1,0:T(8,128)}, f32[2,256,128]{2,1,0:T(8,128)...) custom-call(bf16[2,272,1024]{2,1,0:T(8,128)(2,1)} %get-tuple-element.95.proj_ref, ...), custom_call_target="tpu_custom_call" | custom-call | flops 3000000000 | bytes 10334208 | tf_op jit(solution)/shard_map/delta_back_early/pallas_call | solution.py:539
  244.2 12.9 %collective-permute-done.17.far_ref = bf16[4,128,256]{2,1,0:T(8,128)(2,1)S(1)} collective-permute-done((bf16[4,128,256]{2,1,0:T(8,128)(2,1)}, bf16[4,128,256]{2,1,0:T(8,128)(2,1)S(1)}, u32[]{:S(2)}, u32[]{:S(2)}) %collective-permute-start.17) | collective-permute-done | bytes 262176 | tf_op jit(solution)/shard_map/ppermute | solution.py:570
  257.8 2.2 exit.1
  260.0 10.9 %delta_back_late.1 = (f32[2,272,1024]{2,1,0:T(8,128)}, bf16[2,256,128]{2,1,0:T(8,128)(2,1)}, f32[4,768]{1,0:T(4,128)}, f32[1,128]{1,0:T(1,128)}) custom-call(bf16[2,272,1024]{2,1,0:T(8,128)(2,1)} %get-tuple-element.95.proj_ref, f32[2,256,128]{2,1,0:T(8,128)} %get-tuple-element.96.gates_ref, f32[2,256,128]{2,1,0:T(8,128)} %get-tuple-element.81.sums_ref, ...), custom_call_target="tpu_custom_call" | custom-call | flops 3000000000 | bytes 10084864 | tf_op jit(solution)/shard_map/delta_back_late/pallas_call | solution.py:539
  271.8 1.3 collective-permute-start.18
  273.1 7.6 %collective-permute-done.18.edge_ref = f32[2,16,1024]{2,1,0:T(8,128)S(1)} collective-permute-done((f32[2,16,1024]{2,1,0:T(8,128)S(1)}, f32[2,16,1024]{2,1,0:T(8,128)S(1)}, u32[]{:S(2)}, u32[]{:S(2)}) %collective-permute-start.18) | collective-permute-done | bytes 131104 | tf_op jit(solution)/shard_map/ppermute | solution.py:570
  281.3 5.8 %input_back.1 = (bf16[2,256,1024]{2,1,0:T(8,128)(2,1)}, bf16[2,256,1024]{2,1,0:T(8,128)(2,1)}) custom-call(f32[2,272,1024]{2,1,0:T(8,128)} %get-tuple-element.121.dext_ref, f32[2,16,1024]{2,1,0:T(8,128)} %copy-done.16, bf16[2,256,512]{2,1,0:T(8,128)(2,1)} %get-tuple-element.122.dpg_ref, bf16[2,256,128]{2,1,0:T(8,128)(2,1)} %get-tuple-element.123.dgates_ref, ...), custom_call_target="tpu_custom_call" | custom-call | flops 1700000000 | bytes 8519680 | tf_op jit(solution)/shard_map/input_back/pallas_call | solution.py:539
  287.1 5.1 bitcast_convert_fusion.1
  292.5 1.5 copy-done.28
  293.9 6.6 %bitcast_convert_fusion = bf16[1024,2816]{1,0:T(8,128)(2,1)} fusion(bf16[2,256,1024]{2,1,0:T(8,128)(2,1)} %get-tuple-element.137, bf16[2,256,2816]{2,1,0:T(8,128)(2,1)S(1)} %copy-done.28), kind=kOutput, calls=%fused_computation | convolution fusion | flops 2955673600 | bytes 9699328 | tf_op jit(solution)/shard_map/spa,spb->ab/dot_general | solution.py:754
  302.4 2.2 collective-permute-done.7
  304.6 2.7 add_convert_fusion
  307.4 1.5 convert_bitcast_fusion.1
  308.9 4.2 first_norm_back.1
  313.8 76.4 %psum.7 = f32[6528]{0:T(1024)S(1)} all-reduce(f32[6528]{0:T(1024)S(1)} %constant_dynamic-update-slice_fusion), channel_id=1, replica_groups=mesh['seq'=16,'head'=2] {'seq'}, use_global_device_ids=true, to_apply=%region_2.3 | all-reduce | flops 6528 | bytes 52224 | tf_op jit(solution)/shard_map/psum | solution.py:772
  396.5 24.9 %reduce-scatter.7.cloned.1.call-done = bf16[64,1664]{1,0:T(8,128)(2,1)} async-done(((bf16[1024,1664]{1,0:T(8,128)(2,1)}), bf16[64,1664]{1,0:T(8,128)(2,1)}) %reduce-scatter.7.cloned.1.call-update) | async-done | bytes 213008 | tf_op jit(solution)/shard_map/reduce_scatter | solution.py:757
  422.8 1.4 fusion.11
  424.2 1.6 fusion.10
  425.8 122.6 %reduce-scatter.11.cloned.1.call-done = bf16[64,2816]{1,0:T(8,128)(2,1)} async-done(((bf16[1024,2816]{1,0:T(8,128)(2,1)}), bf16[64,2816]{1,0:T(8,128)(2,1)}) %reduce-scatter.11.cloned.1.call-update) | async-done | bytes 360464 | tf_op jit(solution)/shard_map/reduce_scatter | solution.py:757
  548.4 1.9 fusion.9
  (136 shorter events, 33.3 us)
Async XLA Ops:
  7.2 300.2 %reduce-scatter.9.cloned.1.call-start = ((), (), s32[]{:S(2)}) async-start(), calls=%async_computation.5 | async-start | bytes 1114112 | tf_op jit(solution)/shard_map/reduce_scatter | solution.py:757
  8.1 8.6 %collective-permute-start = (bf16[2,16,1024]{2,1,0:T(8,128)(2,1)S(1)}, bf16[2,16,1024]{2,1,0:T(8,128)(2,1)S(1)}, u32[]{:S(2)}, u32[]{:S(2)}) collective-permute-start(bf16[2,16,1024]{2,1,0:T(8,128)(2,1)S(1)} %slice.73), channel_id=1, source_target_pairs={{0,2},{2,4},{4,6},{6,8},{8,10},{10,12},{12,14},{14,16},{16,18},{18... | collective-permute-start | bytes 196616 | tf_op jit(solution)/shard_map/ppermute | solution.py:570
  38.2 45.4 %collective-permute-start.1 = (bf16[4,128,384]{2,1,0:T(8,128)(2,1)}, bf16[4,128,384]{2,1,0:T(8,128)(2,1)S(1)}, u32[]{:S(2)}, u32[]{:S(2)}) collective-permute-start(bf16[4,128,384]{2,1,0:T(8,128)(2,1)} %bitcast.96), channel_id=1, source_target_pairs={{0,2},{2,4},{4,6},{6,8},{8,10},{10,12},{12,14},{14,16},{16,18},{18... | collective-permute-start | bytes 1179656 | tf_op jit(solution)/shard_map/ppermute | solution.py:570
  83.6 0.8 copy-start.4
  87.0 6.9 %collective-permute-start.2 = (bf16[4,128,384]{2,1,0:T(8,128)(2,1)}, bf16[4,128,384]{2,1,0:T(8,128)(2,1)S(1)}, u32[]{:S(2)}, u32[]{:S(2)}) collective-permute-start(bf16[4,128,384]{2,1,0:T(8,128)(2,1)} %get-tuple-element.83), channel_id=1, source_target_pairs={{0,4},{2,6},{4,8},{6,10},{8,12},{10,14},{12,16},{14,18},{16,20},{1... | collective-permute-start | bytes 1179656 | tf_op jit(solution)/shard_map/ppermute | solution.py:570
  93.9 0.8 copy-start.6
  97.3 7.8 %collective-permute-start.3 = (bf16[4,128,384]{2,1,0:T(8,128)(2,1)}, bf16[4,128,384]{2,1,0:T(8,128)(2,1)S(1)}, u32[]{:S(2)}, u32[]{:S(2)}) collective-permute-start(bf16[4,128,384]{2,1,0:T(8,128)(2,1)} %get-tuple-element.85), channel_id=1, source_target_pairs={{0,8},{2,10},{4,12},{6,14},{8,16},{10,18},{12,20},{14,22},{16,24},... | collective-permute-start | bytes 1179656 | tf_op jit(solution)/shard_map/ppermute | solution.py:570
  105.1 0.8 copy-start.7
  108.5 12.6 %collective-permute-start.4 = (bf16[4,128,384]{2,1,0:T(8,128)(2,1)}, bf16[4,128,384]{2,1,0:T(8,128)(2,1)S(1)}, u32[]{:S(2)}, u32[]{:S(2)}) collective-permute-start(bf16[4,128,384]{2,1,0:T(8,128)(2,1)} %get-tuple-element.86), channel_id=1, source_target_pairs={{0,2},{2,4},{4,6},{6,8},{8,10},{10,12},{12,14},{14,16},{16,18},{18... | collective-permute-start | bytes 1179656 | tf_op jit(solution)/shard_map/ppermute | solution.py:570
  110.8 10.3 %collective-permute-start.5 = (bf16[4,128,256]{2,1,0:T(8,128)(2,1)S(1)}, bf16[4,128,256]{2,1,0:T(8,128)(2,1)S(1)}, u32[]{:S(2)}, u32[]{:S(2)}) collective-permute-start(bf16[4,128,256]{2,1,0:T(8,128)(2,1)S(1)} %slice.75), channel_id=1, source_target_pairs={{0,18},{2,20},{4,22},{6,24},{8,26},{10,28},{12,30},{1,19},{3,21},{... | collective-permute-start | bytes 786440 | tf_op jit(solution)/shard_map/ppermute | solution.py:570
  121.1 0.7 copy-start.12
  121.8 0.7 copy-start.5
  129.7 2.9 collective-permute-start.6
  132.6 1.0 copy-start.21
  149.9 2.9 collective-permute-start.12
  152.8 1.0 copy-start.2
  153.8 7.5 %copy-start.22 = (bf16[2,256,512]{2,1,0:T(8,128)(2,1)S(1)}, bf16[2,256,512]{2,1,0:T(8,128)(2,1)}, u32[]{:S(2)}) copy-start(bf16[2,256,512]{2,1,0:T(8,128)(2,1)} %get-tuple-element.136) | copy-start | bytes 1572868
  164.4 230.0 %reduce-scatter.13.cloned.1.call-start = ((), (), s32[]{:S(2)}) async-start(), calls=%async_computation.7 | async-start | bytes 3063808
  170.7 0.9 copy-start.23
  170.7 250.7 %reduce-scatter.7.cloned.1.call-start = ((), (), s32[]{:S(2)}) async-start(), calls=%async_computation.4 | async-start | bytes 3620864 | tf_op jit(solution)/shard_map/reduce_scatter | solution.py:757
  171.6 14.2 %collective-permute-start.13 = (bf16[4,128,256]{2,1,0:T(8,128)(2,1)S(1)}, bf16[4,128,256]{2,1,0:T(8,128)(2,1)S(1)}, u32[]{:S(2)}, u32[]{:S(2)}) collective-permute-start(bf16[4,128,256]{2,1,0:T(8,128)(2,1)S(1)} %bitcast.113), channel_id=1, source_target_pairs={{2,0},{4,2},{6,4},{8,6},{10,8},{12,10},{14,12},{16,14},{18,16},{20... | collective-permute-start | bytes 786440 | tf_op jit(solution)/shard_map/ppermute | solution.py:570
  185.8 0.7 copy-start.13
  188.9 16.9 %collective-permute-start.14 = (bf16[4,128,256]{2,1,0:T(8,128)(2,1)}, bf16[4,128,256]{2,1,0:T(8,128)(2,1)S(1)}, u32[]{:S(2)}, u32[]{:S(2)}) collective-permute-start(bf16[4,128,256]{2,1,0:T(8,128)(2,1)} %get-tuple-element.107), channel_id=1, source_target_pairs={{4,0},{6,2},{8,4},{10,6},{12,8},{14,10},{16,12},{18,14},{20,16},{2... | collective-permute-start | bytes 786440 | tf_op jit(solution)/shard_map/ppermute | solution.py:570
  191.1 10.8 %collective-permute-start.8 = (bf16[4,128,128]{2,1,0:T(8,128)(2,1)S(1)}, bf16[4,128,128]{2,1,0:T(8,128)(2,1)S(1)}, u32[]{:S(2)}, u32[]{:S(2)}) collective-permute-start(bf16[4,128,128]{2,1,0:T(8,128)(2,1)S(1)} %slice.95), channel_id=1, source_target_pairs={{2,0},{4,2},{6,4},{8,6},{10,8},{12,10},{14,12},{16,14},{18,16},{20... | collective-permute-start | bytes 393224 | tf_op jit(solution)/shard_map/ppermute | solution.py:570
  201.9 0.7 copy-start.25
  204.6 7.9 %collective-permute-start.9 = (bf16[4,128,128]{2,1,0:T(8,128)(2,1)}, bf16[4,128,128]{2,1,0:T(8,128)(2,1)S(1)}, u32[]{:S(2)}, u32[]{:S(2)}) collective-permute-start(bf16[4,128,128]{2,1,0:T(8,128)(2,1)} %get-tuple-element.98), channel_id=1, source_target_pairs={{4,0},{6,2},{8,4},{10,6},{12,8},{14,10},{16,12},{18,14},{20,16},{2... | collective-permute-start | bytes 393224 | tf_op jit(solution)/shard_map/ppermute | solution.py:570
  205.9 0.7 copy-start.9
  209.0 20.1 %collective-permute-start.15 = (bf16[4,128,256]{2,1,0:T(8,128)(2,1)}, bf16[4,128,256]{2,1,0:T(8,128)(2,1)S(1)}, u32[]{:S(2)}, u32[]{:S(2)}) collective-permute-start(bf16[4,128,256]{2,1,0:T(8,128)(2,1)} %get-tuple-element.109), channel_id=1, source_target_pairs={{8,0},{10,2},{12,4},{14,6},{16,8},{18,10},{20,12},{22,14},{24,16},... | collective-permute-start | bytes 786440 | tf_op jit(solution)/shard_map/ppermute | solution.py:570
  212.4 0.7 copy-start.24
  215.1 10.1 %collective-permute-start.10 = (bf16[4,128,128]{2,1,0:T(8,128)(2,1)}, bf16[4,128,128]{2,1,0:T(8,128)(2,1)S(1)}, u32[]{:S(2)}, u32[]{:S(2)}) collective-permute-start(bf16[4,128,128]{2,1,0:T(8,128)(2,1)} %get-tuple-element.100), channel_id=1, source_target_pairs={{8,0},{10,2},{12,4},{14,6},{16,8},{18,10},{20,12},{22,14},{24,16},... | collective-permute-start | bytes 393224 | tf_op jit(solution)/shard_map/ppermute | solution.py:570
  225.2 0.7 copy-start.26
  227.8 15.4 %collective-permute-start.11 = (bf16[4,128,128]{2,1,0:T(8,128)(2,1)}, bf16[4,128,128]{2,1,0:T(8,128)(2,1)S(1)}, u32[]{:S(2)}, u32[]{:S(2)}) collective-permute-start(bf16[4,128,128]{2,1,0:T(8,128)(2,1)} %get-tuple-element.101), channel_id=1, source_target_pairs={{2,0},{4,2},{6,4},{8,6},{10,8},{12,10},{14,12},{16,14},{18,16},{20... | collective-permute-start | bytes 393224 | tf_op jit(solution)/shard_map/ppermute | solution.py:570
  229.1 0.7 copy-start.8
  232.2 11.9 %collective-permute-start.16 = (bf16[4,128,256]{2,1,0:T(8,128)(2,1)}, bf16[4,128,256]{2,1,0:T(8,128)(2,1)S(1)}, u32[]{:S(2)}, u32[]{:S(2)}) collective-permute-start(bf16[4,128,256]{2,1,0:T(8,128)(2,1)} %get-tuple-element.110), channel_id=1, source_target_pairs={{2,0},{4,2},{6,4},{8,6},{10,8},{12,10},{14,12},{16,14},{18,16},{20... | collective-permute-start | bytes 786440 | tf_op jit(solution)/shard_map/ppermute | solution.py:570
  233.5 23.6 %collective-permute-start.17 = (bf16[4,128,256]{2,1,0:T(8,128)(2,1)}, bf16[4,128,256]{2,1,0:T(8,128)(2,1)S(1)}, u32[]{:S(2)}, u32[]{:S(2)}) collective-permute-start(bf16[4,128,256]{2,1,0:T(8,128)(2,1)} %get-tuple-element.110), channel_id=1, source_target_pairs={{18,0},{20,2},{22,4},{24,6},{26,8},{28,10},{30,12},{19,1},{21,3},{... | collective-permute-start | bytes 786440 | tf_op jit(solution)/shard_map/ppermute | solution.py:570
  243.2 13.9 %copy-start.14 = (bf16[4,128,128]{2,1,0:T(8,128)(2,1)}, bf16[4,128,128]{2,1,0:T(8,128)(2,1)S(1)}, u32[]{:S(2)}) copy-start(bf16[4,128,128]{2,1,0:T(8,128)(2,1)S(1)} %collective-permute-done.11.map_ref) | copy-start | bytes 393220
  244.2 13.0 %copy-start.10 = (bf16[4,128,256]{2,1,0:T(8,128)(2,1)}, bf16[4,128,256]{2,1,0:T(8,128)(2,1)S(1)}, u32[]{:S(2)}) copy-start(bf16[4,128,256]{2,1,0:T(8,128)(2,1)S(1)} %collective-permute-done.16.near_ref) | copy-start | bytes 786436
  257.1 0.7 copy-start.11
  271.8 8.9 %collective-permute-start.18 = (f32[2,16,1024]{2,1,0:T(8,128)S(1)}, f32[2,16,1024]{2,1,0:T(8,128)S(1)}, u32[]{:S(2)}, u32[]{:S(2)}) collective-permute-start(f32[2,16,1024]{2,1,0:T(8,128)S(1)} %slice.78), channel_id=1, source_target_pairs={{2,0},{4,2},{6,4},{8,6},{10,8},{12,10},{14,12},{16,14},{18,16},{20... | collective-permute-start | bytes 393224 | tf_op jit(solution)/shard_map/ppermute | solution.py:570
  280.6 0.7 copy-start.16
  281.3 5.8 %copy-start.3 = (bf16[2,256,512]{2,1,0:T(8,128)(2,1)S(1)}, bf16[2,256,512]{2,1,0:T(8,128)(2,1)}, u32[]{:S(2)}) copy-start(bf16[2,256,512]{2,1,0:T(8,128)(2,1)} %get-tuple-element.122.dpg_ref) | copy-start | bytes 1572868
  281.3 5.8 %copy-start.15 = (bf16[2,256,128]{2,1,0:T(8,128)(2,1)S(1)}, bf16[2,256,128]{2,1,0:T(8,128)(2,1)}, u32[]{:S(2)}) copy-start(bf16[2,256,128]{2,1,0:T(8,128)(2,1)} %get-tuple-element.123.dgates_ref) | copy-start | bytes 393220
  281.3 5.8 %copy-start.29 = (bf16[2,256,1024]{2,1,0:T(8,128)(2,1)S(1)}, bf16[2,256,1024]{2,1,0:T(8,128)(2,1)}, u32[]{:S(2)}) copy-start(bf16[2,256,1024]{2,1,0:T(8,128)(2,1)} %get-tuple-element.127) | copy-start | bytes 3145732
  292.1 1.8 copy-start.28
  292.1 256.2 %reduce-scatter.11.cloned.1.call-start = ((), (), s32[]{:S(2)}) async-start(), calls=%async_computation.6 | async-start | bytes 6127616 | tf_op jit(solution)/shard_map/reduce_scatter | solution.py:757
  300.5 1.2 copy-start.1
  300.5 1.2 copy-start.20
  300.5 1.7 copy-start.19
  300.5 4.0 copy-start
  301.8 2.8 collective-permute-start.7
  301.8 5.5 collective-permute-start.20
  302.3 5.0 copy-start.17
  302.3 5.0 copy-start.27
  302.3 6.6 %collective-permute-start.19 = (bf16[2,256,1024]{2,1,0:T(8,128)(2,1)}, bf16[2,256,1024]{2,1,0:T(8,128)(2,1)}, u32[]{:S(2)}, u32[]{:S(2)}) collective-permute-start(bf16[2,256,1024]{2,1,0:T(8,128)(2,1)} %get-tuple-element.124.mine_ref), channel_id=1, source_target_pairs={{0,1},{1,0},{2,3},{3,2},{4,5},{5,4},{6,7},{7,6},{8,9},{9,8},{10,11... | collective-permute-start | bytes 3145736 | tf_op jit(solution)/shard_map/ppermute | solution.py:575
  308.9 4.9 copy-start.18
Sparse Core Ops, SparseCore 0:
  164.5 84.8 reduce-scatter.8
  251.8 83.8 reduce-scatter.12
  338.1 83.2 reduce-scatter.6
  423.6 124.7 reduce-scatter.10

commit v2 on v1

--- a/solution.py
+++ b/solution.py
@@ -18,6 +18,7 @@
 NN = ((1,), (0,))
 NT = ((1,), (1,))
 TN = ((0,), (0,))
+NOTE = 16
 VMEM_LIMIT = 56 * 1024 * 1024
 
 
@@ -117,14 +118,15 @@
 
 def first_body(
     heads, x_ref, gain_ref, wq_ref, wk_ref, wv_ref, wg_ref, wgates_ref, bias_ref, cq_ref, ck_ref,
-    cv_ref, mixed_ref, proj_ref, pg_ref, gates_ref, sums_ref, inv_ref, mapk_ref, fresh_ref,
-    score_ref, reach_ref, local_ref, decay_ref, piece_ref, low_ref,
+    cv_ref, proj_ref, pg_ref, gates_ref, sums_ref, inv_ref, mapk_ref, fresh_ref,
+    score_ref, reach_ref, local_ref, decay_ref, piece_ref, low_ref, map_ref, maplow_ref, log_ref,
+    turned_ref,
 ):
     x = x_ref[0].astype(F32)
     mixed = x * lax.rsqrt(jnp.mean(x * x, axis=-1, keepdims=True) + 1e-06) * gain_ref[...]
     mixed = mixed.astype(BF16)
     main = mixed[HALO:]
-    mixed_ref[0] = main
+    turned_ref[...] = jnp.transpose(main)
     proj_q = dot(mixed, wq_ref[...]).astype(BF16)
     proj_k = dot(mixed, wk_ref[...]).astype(BF16)
     proj_v = dot(mixed, wv_ref[...]).astype(BF16)
@@ -173,8 +175,14 @@
     for h in each:
         piece_ref[0, h, :, :DK] = moved[h]
         piece_ref[0, h, :, DK:] = shift[h]
-        low_ref[0, h, :, :DK] = moved[h].astype(BF16)
-        low_ref[0, h, :, DK:] = shift[h].astype(BF16)
+        map_ref[0, h] = moved[h]
+        note = log_rows(last[h])
+        log_ref[0, h] = jnp.broadcast_to(last[h], (8, LANES))
+        maplow_ref[0, h, :DK] = moved[h].astype(BF16)
+        maplow_ref[0, h, DK:] = note
+        low_ref[0, h, :DK, :DK] = moved[h].astype(BF16)
+        low_ref[0, h, :DK, DK:] = shift[h].astype(BF16)
+        low_ref[0, h, DK:] = jnp.concatenate([note] * (1 + DV // DK), axis=1)
         inv_ref[0, h] = inverses[h]
         mapk_ref[0, h] = mapk[h]
         fresh_ref[0, h] = fresh[h]
@@ -184,54 +192,85 @@
         decay_ref[0, h] = decay[h]
 
 
-def join_body(pairs, level, piece_ref, got_ref, scale_ref, out_ref, low_ref):
+def log_rows(log):
+    log = jnp.broadcast_to(log, (1, LANES))
+    high = log.astype(BF16).astype(F32)
+    middle = (log - high).astype(BF16).astype(F32)
+    rest = log - high - middle
+    place = lax.broadcasted_iota(jnp.int32, (NOTE, LANES), 0)
+    zero = jnp.zeros((NOTE, LANES), F32)
+    rows = jnp.where(place == 0, high, jnp.where(place == 1, middle, jnp.where(place == 2, rest, zero)))
+    return rows.astype(BF16)
+
+
+def log_of(rows):
+    return jnp.sum(rows.astype(F32), axis=0, keepdims=True)
+
+
+def join_body(pairs, last, piece_ref, log_ref, got_ref, out_ref, newlog_ref, low_ref, *far_ref):
+    wide = 1 + DV // DK
     for p in range(pairs):
         own = piece_ref[p]
-        got = got_ref[p].astype(F32)
-        mine = scale_ref[level, p]
-        theirs = scale_ref[level, pairs + p]
+        got_low = got_ref[p, :DK]
+        got = got_low.astype(F32)
+        own_log = log_ref[p, :1]
+        got_log = log_of(got_ref[p, DK:, :LANES])
+        mine = jnp.concatenate([jnp.exp(own_log)] * wide, axis=1)
         high, low = halves(own[:, :DK])
-        moved = dot(high, got_ref[p]) + dot(low, got_ref[p])
-        moved = moved + mine * got
-        out = jnp.concatenate([moved[:, :DK] + theirs * own[:, :DK], moved[:, DK:] + own[:, DK:]], axis=1)
-        out_ref[p] = out
-        low_ref[p] = out.astype(BF16)
-
-
-def map_body(pairs, level, own_ref, got_ref, scale_ref, out_ref, low_ref):
+        moved = dot(high, got_low) + dot(low, got_low) + mine * got
+        map_part = moved[:, :DK] + jnp.exp(got_log) * own[:, :DK]
+        shift_part = moved[:, DK:] + own[:, DK:]
+        new_log = own_log + got_log
+        out_ref[p, :, :DK] = map_part
+        out_ref[p, :, DK:] = shift_part
+        newlog_ref[p] = jnp.broadcast_to(new_log, (8, LANES))
+        low_ref[p, :DK, :DK] = map_part.astype(BF16)
+        low_ref[p, :DK, DK:] = shift_part.astype(BF16)
+        low_ref[p, DK:] = jnp.concatenate([log_rows(new_log)] * wide, axis=1)
+        if last:
+            far_ref[0][p] = shift_part.astype(BF16)
+
+
+def map_body(pairs, own_ref, log_ref, got_ref, out_ref, newlog_ref, low_ref):
     for p in range(pairs):
         own = own_ref[p]
-        got = got_ref[p]
+        got_low = got_ref[p, :DK]
+        own_log = log_ref[p, :1]
+        got_log = log_of(got_ref[p, DK:])
         high, low = halves(own)
-        out = dot(got, high) + dot(got, low)
-        out = out + scale_ref[level, pairs + p] * own + scale_ref[level, p] * got.astype(F32)
+        out = dot(got_low, high) + dot(got_low, low)
+        out = out + jnp.exp(got_log) * own + jnp.exp(own_log) * got_low.astype(F32)
+        new_log = own_log + got_log
         out_ref[p] = out
-        low_ref[p] = out.astype(BF16)
-
-
-def entry_body(pairs, level, near_ref, far_ref, scale_ref, out_ref):
+        newlog_ref[p] = jnp.broadcast_to(new_log, (8, LANES))
+        low_ref[p, :DK] = out.astype(BF16)
+        low_ref[p, DK:] = log_rows(new_log)
+
+
+def entry_body(pairs, near_ref, far_ref, out_ref):
     for p in range(pairs):
-        near = near_ref[p]
         far = far_ref[p]
-        moved = dot(near[:, :DK], far) + scale_ref[level, p] * far.astype(F32)
-        out_ref[p] = moved + near[:, DK:].astype(F32)
-
-
-def back_body(pairs, level, map_ref, own_ref, got_ref, scale_ref, out_ref, low_ref):
+        scale = jnp.exp(log_of(near_ref[p, DK:, DK:]))
+        moved = dot(near_ref[p, :DK, :DK], far) + scale * far.astype(F32)
+        out_ref[p] = moved + near_ref[p, :DK, DK:].astype(F32)
+
+
+def back_body(pairs, map_ref, log_ref, own_ref, got_ref, out_ref, low_ref):
     for p in range(pairs):
         got = got_ref[p]
         high, low = halves(map_ref[p])
-        moved = dot(high, got, TN) + dot(low, got, TN)
-        out = own_ref[p] + moved + scale_ref[level, p] * got.astype(F32)
+        scale = jnp.concatenate([jnp.exp(log_ref[p, :1])] * (DV // DK), axis=1)
+        out = own_ref[p] + dot(high, got, TN) + dot(low, got, TN) + scale * got.astype(F32)
         out_ref[p] = out
         low_ref[p] = out.astype(BF16)
 
 
-def exit_body(pairs, level, map_ref, near_ref, far_ref, scale_ref, out_ref):
+def exit_body(pairs, map_ref, near_ref, far_ref, out_ref):
     for p in range(pairs):
         far = far_ref[p]
-        moved = dot(map_ref[p], far, TN)
-        out_ref[p] = near_ref[p].astype(F32) + moved + scale_ref[level, p] * far.astype(F32)
+        scale = jnp.concatenate([jnp.exp(log_of(map_ref[p, DK:]))] * (DV // DK), axis=1)
+        moved = dot(map_ref[p, :DK], far, TN) + scale * far.astype(F32)
+        out_ref[p] = near_ref[p].astype(F32) + moved
 
 
 def mixer_out_body(
@@ -253,7 +292,7 @@
 
 def feed_body(
     x_ref, mine_ref, other_ref, cot_ref, gain_ref, wgate_ref, wup_ref, wdown_ref, resid_ref,
-    normed_ref, hidden_ref, dgu_ref, down_ref, dnorm_ref,
+    hidden_ref, dgu_ref, down_ref, dnorm_ref, normed_ref, cot_turned_ref,
 ):
     units = wgate_ref.shape[1]
     attn = mine_ref[0].astype(F32) + other_ref[0].astype(F32)
@@ -261,7 +300,8 @@
     resid_ref[0] = resid
     normed = resid * lax.rsqrt(jnp.mean(resid * resid, axis=-1, keepdims=True) + 1e-06)
     normed = (normed * gain_ref[...]).astype(BF16)
-    normed_ref[0] = normed
+    normed_ref[...] = jnp.transpose(normed)
+    cot_turned_ref[...] = jnp.transpose(cot_ref[0])
     gate = dot(normed, wgate_ref[...])
     up = dot(normed, wup_ref[...])
     d_hidden = dot(cot_ref[0], wdown_ref[...], NT)
@@ -279,7 +319,7 @@
 
 def mixer_back_body(
     heads, resid_ref, mine_ref, other_ref, cot_ref, output_ref, pg_ref, reach_ref, gain_ref,
-    wout_ref, ogain_ref, dresid_ref, dattn_ref, dout_ref, dpg_ref, back_ref, low_ref, dgain_ref,
+    wout_ref, ogain_ref, dresid_ref, dout_ref, dpg_ref, back_ref, low_ref, dattn_ref, dgain_ref,
     dogain_ref,
 ):
     step = pl.program_id(0)
@@ -295,7 +335,7 @@
     d_resid = d_resid + cot_ref[0].astype(F32)
     dresid_ref[0] = d_resid
     d_attn = d_resid.astype(BF16)
-    dattn_ref[0] = d_attn
+    dattn_ref[...] = jnp.transpose(d_attn)
     d_gated = dot(d_attn, wout_ref[...], NT)
     d_ogain = jnp.zeros((1, DV), F32)
     for h in range(heads):
@@ -484,9 +524,10 @@
 
 
 def input_back_body(
-    dext_ref, edge_ref, dpg_ref, dgates_ref, wq_ref, wk_ref, wv_ref, wg_ref, wgates_ref, dproj_ref,
-    dmixed_ref,
+    dext_ref, edge_ref, dpg_ref, dgates_ref, x_ref, wq_ref, wk_ref, wv_ref, wg_ref, wgates_ref,
+    dproj_ref, dmixed_ref, dgain_ref,
 ):
+    step = pl.program_id(0)
     wide = wq_ref.shape[1]
     own = dext_ref[0, HALO:]
     size = own.shape[0]
@@ -499,26 +540,41 @@
     d_mixed = d_mixed + dot(dpg_ref[0], wg_ref[...], NT)
     d_mixed = d_mixed + dot(dgates_ref[0], wgates_ref[...], NT)
     dmixed_ref[0] = d_mixed.astype(BF16)
-
-
-def last_body(x_ref, mine_ref, other_ref, dresid_ref, gain_ref, grad_ref, dgain_ref):
-    step = pl.program_id(0)
+    x = x_ref[0].astype(F32)
+    unit_x = x * lax.rsqrt(jnp.mean(x * x, axis=-1, keepdims=True) + 1e-06)
+    d_gain = jnp.sum(d_mixed * unit_x, axis=0, keepdims=True)
+
+    @pl.when(step == 0)
+    def _():
+        dgain_ref[...] = d_gain
+
+    @pl.when(step > 0)
+    def _():
+        dgain_ref[...] += d_gain
+
+
+def last_body(x_ref, mine_ref, other_ref, dresid_ref, gain_ref, grad_ref):
     x = x_ref[0].astype(F32)
     inverse = lax.rsqrt(jnp.mean(x * x, axis=-1, keepdims=True) + 1e-06)
     unit_x = x * inverse
     d_mixed = mine_ref[0].astype(F32) + other_ref[0].astype(F32)
-    d_gain = jnp.sum(d_mixed * unit_x, axis=0, keepdims=True)
     d_unit = d_mixed * gain_ref[...]
     back = inverse * (d_unit - unit_x * jnp.mean(d_unit * unit_x, axis=-1, keepdims=True))
     grad_ref[0] = dresid_ref[0] + back
 
-    @pl.when(step == 0)
-    def _():
-        dgain_ref[...] = d_gain
-
-    @pl.when(step > 0)
-    def _():
-        dgain_ref[...] += d_gain
+
+def weight_body(terms, first, blocks, lefts, index_ref, *refs):
+    left_refs, right_refs = refs[:lefts], refs[lefts:-2]
+    out_ref, held = refs[-2:]
+    share = left_refs[0].shape[1]
+    for number, left_ref in enumerate(left_refs):
+        for place in range(blocks):
+            held[number, place * share : (place + 1) * share] = left_ref[index_ref[first + place]]
+    at = 0
+    for left, right, begin, width in terms:
+        product = dot(held[left], right_refs[right][:, begin : begin + width])
+        out_ref[:, at : at + width] = product.astype(out_ref.dtype)
+        at += width
 
 
 def by_seq(shape):
@@ -531,16 +587,18 @@
     return pl.BlockSpec(tuple(shape), lambda s: (0,) * rest)
 
 
-def call(body, name, seqs, parts, shared, outs, sums=(), flops=0):
+def call(body, name, seqs, parts, shared, outs, sums=(), turned=(), flops=0):
     operands = list(parts) + list(shared)
-    out_shape = [jax.ShapeDtypeStruct(shape, kind) for shape, kind in list(outs) + list(sums)]
-    moved = sum(a.size * a.dtype.itemsize for a in operands)
-    moved += sum(a.size * a.dtype.itemsize for a in out_shape)
+    listed = list(outs) + list(turned) + list(sums)
+    out_shape = [jax.ShapeDtypeStruct(shape, kind) for shape, kind in listed]
+    moved = sum(a.size * a.dtype.itemsize for a in operands + out_shape)
     return pl.pallas_call(
         body,
         grid=(seqs,),
         in_specs=[by_seq(a.shape) for a in parts] + [whole(a.shape) for a in shared],
-        out_specs=[by_seq(shape) for shape, _ in outs] + [whole(shape) for shape, _ in sums],
+        out_specs=[by_seq(shape) for shape, _ in outs]
+        + [pl.BlockSpec((shape[0], shape[1] // seqs), lambda s: (0, s)) for shape, _ in turned]
+        + [whole(shape) for shape, _ in sums],
         out_shape=out_shape,
         compiler_params=pltpu.CompilerParams(vmem_limit_bytes=VMEM_LIMIT),
         cost_estimate=pl.CostEstimate(flops=int(flops), bytes_accessed=int(moved), transcendentals=0),
@@ -548,20 +606,68 @@
     )(*operands)
 
 
-def small_call(body, name, arrays, scales, outs):
-    operands = list(arrays) + [scales]
+def small_call(body, name, arrays, outs):
     out_shape = [jax.ShapeDtypeStruct(shape, kind) for shape, kind in outs]
     moved = sum(a.size * a.dtype.itemsize for a in list(arrays) + out_shape)
     return pl.pallas_call(
         body,
-        in_specs=[pl.BlockSpec(memory_space=pltpu.VMEM)] * len(arrays)
-        + [pl.BlockSpec(memory_space=pltpu.SMEM)],
+        in_specs=[pl.BlockSpec(memory_space=pltpu.VMEM)] * len(arrays),
         out_specs=[pl.BlockSpec(memory_space=pltpu.VMEM)] * len(outs),
         out_shape=out_shape,
         compiler_params=pltpu.CompilerParams(vmem_limit_bytes=VMEM_LIMIT),
         cost_estimate=pl.CostEstimate(flops=200_000_000, bytes_accessed=int(moved), transcendentals=0),
         name=name,
-    )(*operands)
+    )(*arrays)
+
+
+def weight_call(name, index, lefts, rights, terms, first, blocks, kind):
+    _, share, tokens = lefts[0].shape
+    columns = sum(width for _, _, _, width in terms)
+    out_shape = jax.ShapeDtypeStruct((blocks * share, columns), kind)
+    operands = list(lefts) + list(rights)
+    moved = sum(a.size * a.dtype.itemsize for a in operands + [out_shape])
+    return pl.pallas_call(
+        functools.partial(weight_body, terms, first, blocks, len(lefts)),
+        in_specs=[pl.BlockSpec(memory_space=pltpu.SMEM)]
+        + [pl.BlockSpec(memory_space=pltpu.VMEM)] * len(operands),
+        out_specs=pl.BlockSpec(memory_space=pltpu.VMEM),
+        out_shape=out_shape,
+        scratch_shapes=[pltpu.VMEM((len(lefts), blocks * share, tokens), BF16)],
+        compiler_params=pltpu.CompilerParams(vmem_limit_bytes=VMEM_LIMIT),
+        cost_estimate=pl.CostEstimate(
+            flops=2 * blocks * share * tokens * columns, bytes_accessed=int(moved), transcendentals=0
+        ),
+        name=name,
+    )(index, *operands)
+
+
+def halving_order(count, first):
+    bits = list(range(count.bit_length() - 1))
+    return bits[first : first + 1] + bits[:first] + bits[first + 1 :]
+
+
+def block_index(order, me):
+    count = 1 << len(order)
+    moved = [
+        sum(((place >> (len(order) - 1 - step)) & 1) << bit for step, bit in enumerate(order))
+        for place in range(count)
+    ]
+    return jnp.bitwise_xor(jnp.array(moved, jnp.int32), me)
+
+
+def traded(block, bit):
+    count = lax.axis_size("seq")
+    return lax.ppermute(block, "seq", [(i, i ^ (1 << bit)) for i in range(count)])
+
+
+def halved(send, keep, order):
+    for step, bit in enumerate(order):
+        got = traded(send, bit).astype(F32)
+        if step + 1 < len(order):
+            half = keep.shape[0] // 2
+            send = (keep[half:] + got[half:]).astype(BF16)
+            keep = keep[:half] + got[:half]
+    return keep + got
 
 
 def passed_along(block, axis, distance):
@@ -599,57 +705,72 @@
     square = (seqs, heads, size, size)
     by_key = (seqs, heads, size, DK)
     by_value = (seqs, heads, size, DV)
+    tokens_here = seqs * size
+    order_a, order_b = halving_order(count, 0), halving_order(count, 1)
+    index_a, index_b = block_index(order_a, me), block_index(order_b, me)
+    turned_shape = (width, tokens_here)
+    share = width // count
+
+    def in_blocks(turned):
+        return turned.reshape(count, share, tokens_here)
+
+    def flat(field):
+        return field.reshape(tokens_here, field.shape[2])
+
     (
-        mixed, proj, proj_g, gates, sums, inv, mapk, fresh, score, reach, local, decay, piece, low,
+        proj, proj_g, gates, sums, inv, mapk, fresh, score, reach, local, decay, piece, low,
+        back_map, back_low, log, mixed_t,
     ) = call(
         functools.partial(first_body, heads), "project_and_local", seqs, [x_ext],
         [mix_row, w_query, w_key, w_value, w_outgate, gates_w, bias, conv_query, conv_key, conv_value],
         [
-            ((seqs, size, width), BF16), ((seqs, size + HALO, proj_wide), BF16),
+            ((seqs, size + HALO, proj_wide), BF16),
             ((seqs, size, out_wide), F32), ((seqs, size, LANES), F32), ((seqs, size, LANES), F32),
             (square, F32), (by_key, F32), (by_value, F32), (square, F32), (by_key, F32),
             (by_value, F32), (square, F32), ((seqs, heads, DK, DK + DV), F32),
-            ((seqs, heads, DK, DK + DV), BF16),
+            ((seqs, heads, DK + NOTE, DK + DV), BF16), ((seqs, heads, DK, DK), F32),
+            ((seqs, heads, DK + NOTE, DK), BF16), ((seqs, heads, 8, LANES), F32),
         ],
+        turned=[(turned_shape, BF16)],
         flops=1e10,
     )
 
-    ended = sums[:, size - 1, heads : 2 * heads].reshape(pairs)
-    all_ended = lax.all_gather(ended, "seq")
-    spans = []
+    piece = piece.reshape(pairs, DK, DK + DV)
+    low = low.reshape(pairs, DK + NOTE, DK + DV)
+    log = log.reshape(pairs, 8, LANES)
+    back_maps = [back_map.reshape(pairs, DK, DK)]
+    back_low = back_low.reshape(pairs, DK + NOTE, DK)
+    back_logs = [log]
+    state_shape = (pairs, DK, DV)
     dists = []
     reach_by = 1
     while reach_by * 2 < count:
         dists.append(reach_by)
         reach_by *= 2
-    for d in dists:
-        spans.append(((me - d + 1, me), (me - 2 * d + 1, me - d)))
-    spans.append(((me - reach_by, me - 1), (me, me - 1)))
-    for d in dists:
-        spans.append(((me, me + d - 1), (me + d, me + 2 * d - 1)))
-    spans.append(((me + 1, me + reach_by), (me, me - 1)))
-    low_end = jnp.stack([jnp.stack([a[0] for a in pair]) for pair in spans])[..., None]
-    high_end = jnp.stack([jnp.stack([a[1] for a in pair]) for pair in spans])[..., None]
-    index = jnp.arange(count)
-    within = ((index >= low_end) & (index <= high_end)).astype(F32)
-    scales = jnp.exp(jnp.sum(within[..., None] * all_ended, axis=2)).reshape(len(spans), 2 * pairs)
-
-    piece = piece.reshape(pairs, DK, DK + DV)
-    low = low.reshape(pairs, DK, DK + DV)
-    back_maps = [piece[:, :, :DK]]
-    back_low = low[:, :, :DK]
-    joined, state_shape = (piece, (pairs, DK, DV))
     for level, d in enumerate(dists):
         got = passed_along(low, "seq", d)
-        joined, low = small_call(
-            functools.partial(join_body, pairs, level), "join", [joined, got], scales,
-            [(piece.shape, F32), (piece.shape, BF16)],
+        got_back = passed_along(back_low, "seq", -d)
+        if level:
+            got, _ = lax.optimization_barrier((got, back_low))
+        last = level + 1 == len(dists)
+        outs = [(piece.shape, F32), (log.shape, F32), (low.shape, BF16)]
+        if last:
+            outs.append((state_shape, BF16))
+        piece, log, low, *far = small_call(
+            functools.partial(join_body, pairs, last), "join", [piece, log, got], outs
         )
+        new_map, new_log, back_low = small_call(
+            functools.partial(map_body, pairs), "join_maps", [back_maps[-1], back_logs[-1], got_back],
+            [(back_maps[0].shape, F32), (log.shape, F32), (back_low.shape, BF16)],
+        )
+        back_maps.append(new_map)
+        back_logs.append(new_log)
     near = passed_along(low, "seq", 1)
-    far = passed_along(low[:, :, DK:], "seq", 1 + reach_by)
+    far = passed_along(far[0], "seq", 1 + reach_by)
+    near_map = passed_along(back_low, "seq", -1)
+    far, _ = lax.optimization_barrier((far, back_low))
     (state,) = small_call(
-        functools.partial(entry_body, pairs, len(dists)), "entry", [near, far], scales,
-        [(state_shape, F32)],
+        functools.partial(entry_body, pairs), "entry", [near, far], [(state_shape, F32)]
     )
     state = state.reshape(seqs, heads, DK, DV)
 
@@ -664,55 +785,69 @@
     )
     attn_other = swapped(attn)
 
-    resid, normed, hidden, d_gu, down, d_norm = call(
+    resid, hidden, d_gu, down, d_norm, normed_t, cot_t = call(
         feed_body, "feed_forward", seqs, [tokens, attn, attn_other, cotangent],
         [ffn_row, w_gate, w_up, w_down],
         [
-            ((seqs, size, width), F32), ((seqs, size, width), BF16), ((seqs, size, units), BF16),
+            ((seqs, size, width), F32), ((seqs, size, units), BF16),
             ((seqs, size, 2 * units), BF16), ((seqs, size, width), BF16),
             ((seqs, size, width), BF16),
         ],
+        turned=[(turned_shape, BF16), (turned_shape, BF16)],
         flops=1.2e10,
     )
     d_norm_other = swapped(d_norm)
     down_other = swapped(down)
 
-    level0 = len(dists) + 1
-    for level, d in enumerate(dists):
-        got = passed_along(back_low, "seq", -d)
-        new_map, back_low = small_call(
-            functools.partial(map_body, pairs, level0 + level), "join_maps", [back_maps[-1], got],
-            scales, [((pairs, DK, DK), F32), ((pairs, DK, DK), BF16)],
-        )
-        back_maps.append(new_map)
-    near_map = passed_along(back_low, "seq", -1)
-
-    d_resid, d_attn, d_out, d_pg, back, low, d_ffn_gain, d_out_gain = call(
+    d_resid, d_out, d_pg, back, low, d_attn_t, d_ffn_gain, d_out_gain = call(
         functools.partial(mixer_back_body, heads), "mixer_back", seqs,
         [resid, d_norm, d_norm_other, cotangent, output, proj_g, reach],
         [ffn_row, w_out, out_row],
         [
-            ((seqs, size, width), F32), ((seqs, size, width), BF16), ((seqs, size, out_wide), F32),
+            ((seqs, size, width), F32), ((seqs, size, out_wide), F32),
             ((seqs, size, out_wide), BF16), ((seqs, heads, DK, DV), F32),
             ((seqs, heads, DK, DV), BF16),
         ],
         [((1, width), F32), ((1, DV), F32)],
+        turned=[(turned_shape, BF16)],
         flops=1.5e9,
     )
+
+    half_units = (units // 2 + LANES - 1) // LANES * LANES
+    blocks = count // 2
+
+    def summed(name, index, order, lefts, rights, terms):
+        send = weight_call(name + "_send", index, lefts, rights, terms, blocks, blocks, BF16)
+        keep = weight_call(name + "_keep", index, lefts, rights, terms, 0, blocks, F32)
+        return halved(send, keep, order)
+
+    normed_b, cot_b = in_blocks(normed_t), in_blocks(cot_t)
+    feed_a = summed(
+        "feed_a", index_a, order_a, [normed_b, cot_b], [flat(d_gu), flat(hidden)],
+        ((0, 0, 0, units), (1, 1, 0, half_units)),
+    )
+    feed_b = summed(
+        "feed_b", index_b, order_b, [normed_b, cot_b], [flat(d_gu), flat(hidden)],
+        ((0, 0, units, units), (1, 1, half_units, units - half_units)),
+    )
+    mixed_b = in_blocks(mixed_t)
+    out_t = summed(
+        "out_grad", index_a, order_a, [in_blocks(d_attn_t)], [flat(gated)], ((0, 0, 0, out_wide),)
+    )
+    grad_g = summed("outgate", index_b, order_b, [mixed_b], [flat(d_pg)], ((0, 0, 0, out_wide),))
 
     back = back.reshape(state_shape)
     low = low.reshape(state_shape)
     for level, d in enumerate(dists):
         got = passed_along(low, "seq", -d)
         back, low = small_call(
-            functools.partial(back_body, pairs, level0 + level), "join_back",
-            [back_maps[level], back, got], scales, [(state_shape, F32), (state_shape, BF16)],
+            functools.partial(back_body, pairs), "join_back",
+            [back_maps[level], back_logs[level], back, got], [(state_shape, F32), (state_shape, BF16)],
         )
     near = passed_along(low, "seq", -1)
     far = passed_along(low, "seq", -1 - reach_by)
     (d_end,) = small_call(
-        functools.partial(exit_body, pairs, level0 + len(dists)), "exit", [near_map, near, far],
-        scales, [(state_shape, F32)],
+        functools.partial(exit_body, pairs), "exit", [near_map, near, far], [(state_shape, F32)]
     )
     d_end = d_end.reshape(seqs, heads, DK, DV)
 
@@ -737,55 +872,53 @@
         flops=3e9,
     )
     edges = passed_along(d_ext[:, :HALO], "seq", -1)
-    d_proj, d_mixed = call(
-        input_back_body, "input_back", seqs, [d_ext, edges, d_pg, d_gates],
+    d_proj, d_mixed, d_mix_gain = call(
+        input_back_body, "input_back", seqs, [d_ext, edges, d_pg, d_gates, tokens],
         [w_query, w_key, w_value, w_outgate, gates_w],
         [((seqs, size, proj_wide), BF16), ((seqs, size, width), BF16)],
+        [((1, width), F32)],
         flops=1.7e9,
     )
     d_mixed_other = swapped(d_mixed)
-    grad_input, d_mix_gain = call(
+    ins_a = summed(
+        "query_key", index_a, order_a, [mixed_b], [flat(d_proj), flat(d_gates)],
+        ((0, 0, 0, 2 * wide), (0, 1, 0, LANES)),
+    )
+    ins_b = summed(
+        "value", index_b, order_b, [mixed_b], [flat(d_proj)], ((0, 0, 2 * wide, out_wide),)
+    )
+    (grad_input,) = call(
         last_body, "first_norm_back", seqs, [tokens, d_mixed, d_mixed_other, d_resid], [mix_row],
-        [((seqs, size, width), F32)], [((1, width), F32)],
+        [((seqs, size, width), F32)],
     )
     result = (resid + (down.astype(F32) + down_other.astype(F32))).astype(BF16)
 
-    def weight_grad(left, right):
-        return jnp.einsum("spa,spb->ab", left, right, preferred_element_type=F32).astype(BF16)
-
-    def scattered(grad):
-        return lax.psum_scatter(grad, "seq", scatter_dimension=0, tiled=True).astype(F32)
-
-    gate_up = scattered(weight_grad(normed, d_gu))
-    down_t = scattered(weight_grad(cotangent, hidden))
-    out_t = scattered(weight_grad(d_attn, gated))
-    right = jnp.concatenate([d_proj, d_pg, d_gates], axis=2)
-    ins = scattered(weight_grad(mixed, right))
-
-    out_gain_sum = d_out_gain + swapped(d_out_gain)
+    shared = jnp.concatenate([d_out_gain.reshape(-1), d_mix_gain.reshape(-1)])
+    shared = shared + swapped(shared)
     small = jnp.concatenate(
         [
-            dtap_q.reshape(-1), dtap_kv.reshape(-1), d_bias.reshape(-1), out_gain_sum.reshape(-1),
-            d_mix_gain.reshape(-1), d_ffn_gain.reshape(-1),
+            dtap_q.reshape(-1), dtap_kv.reshape(-1), d_bias.reshape(-1), shared,
+            d_ffn_gain.reshape(-1),
         ]
-    )
-    small = lax.psum(small, "seq")
+    ).reshape(-1, LANES)
+    for bit in order_a:
+        small = small + traded(small, bit)
+    small = small.reshape(-1)
     cuts = [0]
     for length in (CONV * wide, CONV * (wide + out_wide), LANES, DV, width, width):
         cuts.append(cuts[-1] + length)
     pieces = [small[a:b] for a, b in zip(cuts[:-1], cuts[1:])]
     taps_kv = pieces[1].reshape(CONV, wide + out_wide)
-    share = width // count
-    g0 = proj_wide + out_wide
-    grad_gates = jnp.swapaxes(ins[:, g0 : g0 + 2 * heads].reshape(share, 2, heads), 0, 1)
+    grad_gates = ins_a[:, 2 * wide : 2 * wide + 2 * heads].reshape(share, 2, heads)
+    grad_down = jnp.concatenate([feed_a[:, units:], feed_b[:, units:]], axis=1)
     return (
         result,
         grad_input,
-        ins[:, :wide],
-        ins[:, wide : 2 * wide],
-        ins[:, 2 * wide : proj_wide],
-        ins[:, proj_wide : proj_wide + out_wide],
-        grad_gates,
+        ins_a[:, :wide],
+        ins_a[:, wide : 2 * wide],
+        ins_b,
+        grad_g,
+        jnp.swapaxes(grad_gates, 0, 1),
         pieces[2][: 2 * heads].reshape(2, heads),
         pieces[0].reshape(CONV, wide),
         taps_kv[:, :wide],
@@ -794,9 +927,9 @@
         jnp.swapaxes(out_t, 0, 1),
         lax.dynamic_slice_in_dim(pieces[4], me * share, share),
         lax.dynamic_slice_in_dim(pieces[5], me * share, share),
-        gate_up[:, :units],
-        gate_up[:, units:],
-        jnp.swapaxes(down_t, 0, 1),
+        feed_a[:, :units],
+        feed_b[:, :units],
+        jnp.swapaxes(grad_down, 0, 1),
     )
 
 

time: 558 us -> 441 us (0.79); the launches traced: 557 us -> 432 us
  blocking collectives: 117 us -> 0 us
  waiting for transfers between devices: 223 us -> 130 us
  starting transfers between devices: 34 us -> 92.6 us
  Pallas kernels: 102 us -> 152 us
  other arithmetic: 7.33 us -> 30.9 us
  matrix products: 17.9 us -> 0 us
  local copies, waits for them, and re-layouts: 41.1 us -> 24.5 us
  between operations: 14.2 us -> 1.83 us
    reduce_scatter x3 -> x0, waiting for transfers between devices: 147 us -> none  [scattered(): lax.psum_scatter(grad, 'seq', scatter_dimension=0, tiled=True).astype(F32)]
    ppermute x0 -> x28, waiting for transfers between devices: none -> 89.7 us  [traded(): return lax.ppermute(block, 'seq', [(i, i ^ 1 << bit) for i in range(count)])]
    psum x1 -> x0, blocking collectives: 76.4 us -> none  [on_device(): small = lax.psum(small, 'seq')]
    ppermute x0 -> x28, starting transfers between devices: none -> 51.8 us  [traded(): return lax.ppermute(block, 'seq', [(i, i ^ 1 << bit) for i in range(count)])]
    pallas_call x0 -> x12, Pallas kernels: none -> 47 us  [weight_call(): pl.pallas_call(functools.partial(weight_body, terms, first, blocks, len(l...]
    all_gather x1 -> x0, blocking collectives: 40.1 us -> none  [on_device(): all_ended = lax.all_gather(ended, 'seq')]
    ppermute x16, waiting for transfers between devices: 68.1 us -> 36.8 us  [passed_along(): return lax.ppermute(block, axis, route)]
    dot_general x4 -> x0, matrix products: 17.9 us -> none  [weight_grad(): jnp.einsum('spa,spb->ab', left, right, preferred_element_type=F32)]
  transfers between devices with their start and end apart: 25 -> 49, of which waited for: 15 -> 19; matrix products, arithmetic and copies ran while one was open for 8% -> 9% of each run, Pallas kernels for 8% -> 23%
where the time goes in v2:
time: 441 us; the launch traced here: 432 us
  Pallas kernels  152 us (34%)
  waiting for transfers between devices  130 us (29%)
  starting transfers between devices  92.6 us (21%)
  other arithmetic  30.9 us (7%)
  local copies, waits for them, and re-layouts  24.5 us (6%)
    ppermute x28, waiting for transfers between devices, traded(): return lax.ppermute(block, 'seq', [(i, i ^ 1 << bit) for i in range(count)])  89.7 us
    pallas_call x8, Pallas kernels, call(): pl.pallas_call(body, grid=(seqs,), in_specs=[by_seq(a.shape) for a in par...  79.4 us
    ppermute x28, starting transfers between devices, traded(): return lax.ppermute(block, 'seq', [(i, i ^ 1 << bit) for i in range(count)])  51.8 us
    pallas_call x12, Pallas kernels, weight_call(): pl.pallas_call(functools.partial(weight_body, terms, first, blocks, len(l...  47 us
    ppermute x16, starting transfers between devices, passed_along(): return lax.ppermute(block, axis, route)  40.1 us
    ppermute x16, waiting for transfers between devices, passed_along(): return lax.ppermute(block, axis, route)  36.8 us
    pallas_call x11, Pallas kernels, small_call(): pl.pallas_call(body, in_specs=[pl.BlockSpec(memory_space=pltpu.VMEM)] * l...  25.7 us
    unnamed x76, local copies, waits for them, and re-layouts  12.7 us
  transfers between devices with their start and end apart: 49, of which 19 were waited for; matrix products, arithmetic and copies ran while one was open for 9% of the time, Pallas kernels for 23%

profile of v2, /device:TPU:0, one launch (start us, length us, event | category | flops | bytes accessed | tf_op | source)
XLA Modules:
  0.0 432.1 jit_solution(16761350931222689361)
XLA Ops:
  1.5 4.8 %collective-permute-start = (bf16[2,16,1024]{2,1,0:T(8,128)(2,1)S(1)}, bf16[2,16,1024]{2,1,0:T(8,128)(2,1)S(1)}, u32[]{:S(2)}, u32[]{:S(2)}) collective-permute-start(bf16[2,16,1024]{2,1,0:T(8,128)(2,1)S(1)} %slice.282), channel_id=1, source_target_pairs={{0,2},{2,4},{4,6},{6,8},{8,10},{10,12},{12,14},{14,16},{16,18},{18... | collective-permute-start | bytes 196616 | tf_op jit(solution)/shard_map/ppermute | solution.py:676
  9.3 2.3 pad_maximum_fusion.x_ref
  11.6 20.1 %project_and_local.1 = (bf16[2,272,1024]{2,1,0:T(8,128)(2,1)}, f32[2,256,512]{2,1,0:T(8,128)}, f32[2,256,128]{2,1,0:T(8,128)}, f32[2,256,128]{2,1,0:T(8,128)}, f...) custom-call(bf16[2,272,1024]{2,1,0:T(8,128)(2,1)} %pad_maximum_fusio, ...), custom_call_target="tpu_custom_call" | custom-call | flops 10000000000 | bytes 16224768 | tf_op jit(solution)/shard_map/project_and_local/pallas_call | solution.py:595
  31.7 3.4 collective-permute-start.1
  35.1 9.4 %collective-permute-done.1.got_ref = bf16[4,144,384]{2,1,0:T(8,128)(2,1)S(1)} collective-permute-done((bf16[4,144,384]{2,1,0:T(8,128)(2,1)}, bf16[4,144,384]{2,1,0:T(8,128)(2,1)S(1)}, u32[]{:S(2)}, u32[]{:S(2)}) %collective-permute-start.1) | collective-permute-done | bytes 442400 | tf_op jit(solution)/shard_map/ppermute | solution.py:676
  45.3 2.7 join.3
  48.0 5.2 %collective-permute-start.2 = (bf16[4,144,384]{2,1,0:T(8,128)(2,1)}, bf16[4,144,384]{2,1,0:T(8,128)(2,1)S(1)}, u32[]{:S(2)}, u32[]{:S(2)}) collective-permute-start(bf16[4,144,384]{2,1,0:T(8,128)(2,1)} %get-tuple-element.95), channel_id=1, source_target_pairs={{0,4},{2,6},{4,8},{6,10},{8,12},{10,14},{12,16},{14,18},{16,20},{1... | collective-permute-start | bytes 1327112 | tf_op jit(solution)/shard_map/ppermute | solution.py:676
  54.5 5.9 %collective-permute-done.3.got_ref = bf16[4,144,128]{2,1,0:T(8,128)(2,1)S(1)} collective-permute-done((bf16[4,144,128]{2,1,0:T(8,128)(2,1)}, bf16[4,144,128]{2,1,0:T(8,128)(2,1)S(1)}, u32[]{:S(2)}, u32[]{:S(2)}) %collective-permute-start.3) | collective-permute-done | bytes 147488 | tf_op jit(solution)/shard_map/ppermute | solution.py:676
  63.9 2.7 join.4
  66.6 4.6 %collective-permute-start.4 = (bf16[4,144,384]{2,1,0:T(8,128)(2,1)}, bf16[4,144,384]{2,1,0:T(8,128)(2,1)S(1)}, u32[]{:S(2)}, u32[]{:S(2)}) collective-permute-start(bf16[4,144,384]{2,1,0:T(8,128)(2,1)} %get-tuple-element.102), channel_id=1, source_target_pairs={{0,8},{2,10},{4,12},{6,14},{8,16},{10,18},{12,20},{14,22},{16,24},... | collective-permute-start | bytes 1327112 | tf_op jit(solution)/shard_map/ppermute | solution.py:676
  72.5 5.9 %collective-permute-done.5.got_ref = bf16[4,144,128]{2,1,0:T(8,128)(2,1)S(1)} collective-permute-done((bf16[4,144,128]{2,1,0:T(8,128)(2,1)}, bf16[4,144,128]{2,1,0:T(8,128)(2,1)S(1)}, u32[]{:S(2)}, u32[]{:S(2)}) %collective-permute-start.5) | collective-permute-done | bytes 147488 | tf_op jit(solution)/shard_map/ppermute | solution.py:676
  81.9 2.8 join.5
  84.6 5.1 %collective-permute-start.6 = (bf16[4,144,384]{2,1,0:T(8,128)(2,1)}, bf16[4,144,384]{2,1,0:T(8,128)(2,1)S(1)}, u32[]{:S(2)}, u32[]{:S(2)}) collective-permute-start(bf16[4,144,384]{2,1,0:T(8,128)(2,1)} %get-tuple-element.107), channel_id=1, source_target_pairs={{0,2},{2,4},{4,6},{6,8},{8,10},{10,12},{12,14},{14,16},{16,18},{18... | collective-permute-start | bytes 1327112 | tf_op jit(solution)/shard_map/ppermute | solution.py:676
  89.8 3.6 collective-permute-start.7
  94.7 5.9 %collective-permute-done.8.got_ref = bf16[4,144,128]{2,1,0:T(8,128)(2,1)S(1)} collective-permute-done((bf16[4,144,128]{2,1,0:T(8,128)(2,1)}, bf16[4,144,128]{2,1,0:T(8,128)(2,1)S(1)}, u32[]{:S(2)}, u32[]{:S(2)}) %collective-permute-start.8) | collective-permute-done | bytes 147488 | tf_op jit(solution)/shard_map/ppermute | solution.py:676
  106.8 5.3 %mixer_out.1 = (f32[2,2,256,256]{3,2,1,0:T(8,128)}, f32[2,256,512]{2,1,0:T(8,128)}, bf16[2,256,512]{2,1,0:T(8,128)(2,1)}, bf16[2,256,1024]{2,1,0:T(8,128)(2,1)}) custom-call(f32[2,2,128,256]{3,2,1,0:T(8,128)} %bitcast.81, f32[2,2,256,256]{3,2,1,0:T(8,128)} %get-tuple-element.113.fresh_ref, f32[2,2,256,128]{3,2,1,0:T(8,128)} %get-tuple-element.114.mapk_ref, ...), custom_call_target="tpu_custom_call" | custom-call | flops 1500000000 | bytes 9438208 | tf_op jit(solution)/shard_map/mixer_out/pallas_call | solution.py:595
  112.1 2.9 collective-permute-done.9.other_ref
  116.0 17.4 %feed_forward.1 = (f32[2,256,1024]{2,1,0:T(8,128)}, bf16[2,256,1408]{2,1,0:T(8,128)(2,1)}, bf16[2,256,2816]{2,1,0:T(8,128)(2,1)}, bf16[2,256,1024]{2,1,0:T(8,128...) custom-call(bf16[2,256,1024]{2,1,0:T(8,128)(2,1)} %x_ref.5, ...), custom_call_target="tpu_custom_call" | custom-call | flops 12000000000 | bytes 23465984 | tf_op jit(solution)/shard_map/feed_forward/pallas_call | solution.py:595
  135.0 5.6 %feed_a_send.1 = bf16[512,2176]{1,0:T(8,128)(2,1)} custom-call(s32[16]{0:T(128)} %broadcast_xor_fusion.1.index_ref, bf16[16,64,512]{2,1,0:T(8,128)(2,1)} %bitcast.69, bf16[16,64,512]{2,1,0:T(8,128)(2,1)} %bitcast.73, bf16[512,2816]{1,0:T(8,128)(2,1)} %bitcast.49, bf16[512,1408]{1,0:T(8,128)(2,1)} %bitcast.59), custom_call_target="tpu_custom_call" | custom-call | flops 1140850688 | bytes 8650752 | tf_op jit(solution)/shard_map/feed_a_send/pallas_call | solution.py:629
  142.1 5.6 %feed_b_send.1 = bf16[512,2048]{1,0:T(8,128)(2,1)} custom-call(s32[16]{0:T(128)} %broadcast_xor_fusion.index_ref, bf16[16,64,512]{2,1,0:T(8,128)(2,1)} %bitcast.70, bf16[16,64,512]{2,1,0:T(8,128)(2,1)} %bitcast.74, bf16[512,2816]{1,0:T(8,128)(2,1)} %bitcast.50, bf16[512,1408]{1,0:T(8,128)(2,1)} %bitcast.60), custom_call_target="tpu_custom_call" | custom-call | flops 1073741824 | bytes 8519680 | tf_op jit(solution)/shard_map/feed_b_send/pallas_call | solution.py:629
  149.0 6.3 %feed_b_keep.1 = f32[512,2048]{1,0:T(8,128)} custom-call(s32[16]{0:T(128)} %broadcast_xor_fusion.index_ref, bf16[16,64,512]{2,1,0:T(8,128)(2,1)} %bitcast.71, bf16[16,64,512]{2,1,0:T(8,128)(2,1)} %bitcast.75, bf16[512,2816]{1,0:T(8,128)(2,1)} %bitcast.51, bf16[512,1408]{1,0:T(8,128)(2,1)} %bitcast.61), custom_call_target="tpu_custom_call" | custom-call | flops 1073741824 | bytes 10616832 | tf_op jit(solution)/shard_map/feed_b_keep/pallas_call | solution.py:629
  155.3 6.4 %feed_a_keep.1 = f32[512,2176]{1,0:T(8,128)} custom-call(s32[16]{0:T(128)} %broadcast_xor_fusion.1.index_ref, bf16[16,64,512]{2,1,0:T(8,128)(2,1)} %bitcast.72, bf16[16,64,512]{2,1,0:T(8,128)(2,1)} %bitcast.76, bf16[512,2816]{1,0:T(8,128)(2,1)} %bitcast.52, bf16[512,1408]{1,0:T(8,128)(2,1)} %bitcast.62), custom_call_target="tpu_custom_call" | custom-call | flops 1140850688 | bytes 10878976 | tf_op jit(solution)/shard_map/feed_a_keep/pallas_call | solution.py:629
  162.7 7.5 %mixer_back.1 = (f32[2,256,1024]{2,1,0:T(8,128)}, f32[2,256,512]{2,1,0:T(8,128)}, bf16[2,256,512]{2,1,0:T(8,128)(2,1)}, f32[2,2,128,256]{3,2,1,0:T(8,128)}, bf16...) custom-call(f32[2,256,1024]{2,1,0:T(8,128)} %get-tuple-element.119.resid_ref, ...), custom_call_target="tpu_custom_call" | custom-call | flops 1500000000 | bytes 14428160 | tf_op jit(solution)/shard_map/mixer_back/pallas_call | solution.py:595
  171.7 2.8 outgate_send.1
  176.6 2.6 out_grad_send.1
  180.5 2.7 add_convert_fusion
  183.2 8.1 %delta_back_early.1 = (f32[2,2,256,256]{3,2,1,0:T(8,128)}, f32[2,2,256,128]{3,2,1,0:T(8,128)}, f32[2,2,256,128]{3,2,1,0:T(8,128)}, f32[2,256,128]{2,1,0:T(8,128)...) custom-call(bf16[2,272,1024]{2,1,0:T(8,128)(2,1)} %get-tuple-element.121.proj_ref, ...), custom_call_target="tpu_custom_call" | custom-call | flops 3000000000 | bytes 10334208 | tf_op jit(solution)/shard_map/delta_back_early/pallas_call | solution.py:595
  192.0 2.8 outgate_keep.1
  194.8 2.9 out_grad_keep.1
  198.4 2.4 join_back.3
  202.1 9.0 %collective-permute-done.28 = bf16[512,512]{1,0:T(8,128)(2,1)} collective-permute-done((bf16[512,512]{1,0:T(8,128)(2,1)}, bf16[512,512]{1,0:T(8,128)(2,1)}, u32[]{:S(2)}, u32[]{:S(2)}) %collective-permute-start.28) | collective-permute-done | bytes 524320 | tf_op jit(solution)/shard_map/ppermute | solution.py:660
  212.5 6.0 %collective-permute-start.29 = (bf16[256,512]{1,0:T(8,128)(2,1)S(1)}, bf16[256,512]{1,0:T(8,128)(2,1)S(1)}, u32[]{:S(2)}, u32[]{:S(2)}) collective-permute-start(bf16[256,512]{1,0:T(8,128)(2,1)S(1)} %get-tuple-element.175), channel_id=1, source_target_pairs={{0,2},{2,0},{4,6},{6,4},{8,10},{10,8},{12,14},{14,12},{16,18},{18,... | collective-permute-start | bytes 786440 | tf_op jit(solution)/shard_map/ppermute | solution.py:660
  218.9 2.5 collective-permute-start.38
  222.1 2.4 join_back.4
  226.0 2.7 collective-permute-start.30
  229.0 6.9 %collective-permute-done.15.got_ref = bf16[4,128,256]{2,1,0:T(8,128)(2,1)S(1)} collective-permute-done((bf16[4,128,256]{2,1,0:T(8,128)(2,1)}, bf16[4,128,256]{2,1,0:T(8,128)(2,1)S(1)}, u32[]{:S(2)}, u32[]{:S(2)}) %collective-permute-start.15) | collective-permute-done | bytes 262176 | tf_op jit(solution)/shard_map/ppermute | solution.py:676
  236.6 2.5 join_back.5
  242.8 12.8 %collective-permute-done.31 = bf16[64,512]{1,0:T(8,128)(2,1)S(1)} collective-permute-done((bf16[64,512]{1,0:T(8,128)(2,1)S(1)}, bf16[64,512]{1,0:T(8,128)(2,1)S(1)}, u32[]{:S(2)}, u32[]{:S(2)}) %collective-permute-start.31) | collective-permute-done | bytes 65568 | tf_op jit(solution)/shard_map/ppermute | solution.py:660
  256.3 4.5 %collective-permute-done.40 = bf16[64,512]{1,0:T(8,128)(2,1)S(1)} collective-permute-done((bf16[64,512]{1,0:T(8,128)(2,1)S(1)}, bf16[64,512]{1,0:T(8,128)(2,1)S(1)}, u32[]{:S(2)}, u32[]{:S(2)}) %collective-permute-start.40) | collective-permute-done | bytes 65568 | tf_op jit(solution)/shard_map/ppermute | solution.py:660
  262.8 2.6 convert_element_type.177
  265.4 2.5 collective-permute-done.11.map_ref
  269.4 2.2 exit.1
  271.6 10.9 %delta_back_late.1 = (f32[2,272,1024]{2,1,0:T(8,128)}, bf16[2,256,128]{2,1,0:T(8,128)(2,1)}, f32[4,768]{1,0:T(4,128)}, f32[1,128]{1,0:T(1,128)}) custom-call(bf16[2,272,1024]{2,1,0:T(8,128)(2,1)} %get-tuple-element.121.proj_ref, f32[2,256,128]{2,1,0:T(8,128)} %get-tuple-element.122.gates_ref, f32[2,256,128]{2,1,0:T(8,128)} %get-tuple-element.123.sums_ref, ...), custom_call_target="tpu_custom_call" | custom-call | flops 3000000000 | bytes 10084864 | tf_op jit(solution)/shard_map/delta_back_late/pallas_call | solution.py:595
  285.0 4.7 %slice_add_fusion.3 = (f32[256,2048]{1,0:T(8,128)}, bf16[256,2048]{1,0:T(8,128)(2,1)}) fusion(f32[512,2048]{1,0:T(8,128)} %convert_element_type.177, f32[512,2048]{1,0:T(8,128)S(1)} %copy-done), kind=kLoop, calls=%fused_computation.5 | loop fusion | flops 1572864 | bytes 11534336 | tf_op jit(solution)/shard_map/add | solution.py:669
  289.7 3.7 collective-permute-start.46
  294.1 6.1 %input_back.1 = (bf16[2,256,1024]{2,1,0:T(8,128)(2,1)}, bf16[2,256,1024]{2,1,0:T(8,128)(2,1)}, f32[1,1024]{1,0:T(1,128)}) custom-call(f32[2,272,1024]{2,1,0:T(8,128)} %get-tuple-element.143.dext_ref, f32[2,16,1024]{2,1,0:T(8,128)} %copy-done.21, bf16[2,256,512]{2,1,0:T(8,128)(2,1)} %get-tuple-element.144.dpg_ref, ...), custom_call_target="tpu_custom_call" | custom-call | flops 1700000000 | bytes 9572352 | tf_op jit(solution)/shard_map/input_back/pallas_call | solution.py:595
  304.6 4.7 %collective-permute-start.42 = (bf16[256,2176]{1,0:T(8,128)(2,1)}, bf16[256,2176]{1,0:T(8,128)(2,1)}, u32[]{:S(2)}, u32[]{:S(2)}) collective-permute-start(bf16[256,2176]{1,0:T(8,128)(2,1)} %get-tuple-element.163), channel_id=1, source_target_pairs={{0,4},{2,6},{4,0},{6,2},{8,12},{10,14},{12,8},{14,10},{16,20},{18,... | collective-permute-start | bytes 3342344 | tf_op jit(solution)/shard_map/ppermute | solution.py:660
  309.3 5.1 %collective-permute-done.33 = f32[51,128]{1,0:T(8,128)S(1)} collective-permute-done((f32[51,128]{1,0:T(8,128)S(1)}, f32[51,128]{1,0:T(8,128)S(1)}, u32[]{:S(2)}, u32[]{:S(2)}) %collective-permute-start.33) | collective-permute-done | bytes 26144 | tf_op jit(solution)/shard_map/ppermute | solution.py:660
  314.4 3.2 collective-permute-start.34
  317.6 3.0 query_key_send.1
  320.6 14.1 %collective-permute-done.34 = f32[51,128]{1,0:T(8,128)S(1)} collective-permute-done((f32[51,128]{1,0:T(8,128)S(1)}, f32[51,128]{1,0:T(8,128)S(1)}, u32[]{:S(2)}, u32[]{:S(2)}) %collective-permute-start.34) | collective-permute-done | bytes 26144 | tf_op jit(solution)/shard_map/ppermute | solution.py:660
  334.7 2.9 collective-permute-start.35
  337.6 3.2 query_key_keep.1
  341.0 2.8 value_send.1
  344.1 3.0 value_keep.1
  351.6 9.9 %collective-permute-done.24 = bf16[512,512]{1,0:T(8,128)(2,1)} collective-permute-done((bf16[512,512]{1,0:T(8,128)(2,1)}, bf16[512,512]{1,0:T(8,128)(2,1)}, u32[]{:S(2)}, u32[]{:S(2)}) %collective-permute-start.24) | collective-permute-done | bytes 524320 | tf_op jit(solution)/shard_map/ppermute | solution.py:660
  366.3 4.2 collective-permute-done.25
  376.5 3.0 collective-permute-start.27
  379.7 8.6 %collective-permute-done.27 = bf16[64,512]{1,0:T(8,128)(2,1)S(1)} collective-permute-done((bf16[64,512]{1,0:T(8,128)(2,1)S(1)}, bf16[64,512]{1,0:T(8,128)(2,1)S(1)}, u32[]{:S(2)}, u32[]{:S(2)}) %collective-permute-start.27) | collective-permute-done | bytes 65568 | tf_op jit(solution)/shard_map/ppermute | solution.py:660
  388.9 4.1 first_norm_back.1
  394.5 3.4 collective-permute-start.23
  403.5 3.4 collective-permute-start.48
  406.9 9.8 %collective-permute-done.43 = bf16[128,2176]{1,0:T(8,128)(2,1)S(1)} collective-permute-done((bf16[128,2176]{1,0:T(8,128)(2,1)}, bf16[128,2176]{1,0:T(8,128)(2,1)S(1)}, u32[]{:S(2)}, u32[]{:S(2)}) %collective-permute-start.43) | collective-permute-done | bytes 557088 | tf_op jit(solution)/shard_map/ppermute | solution.py:660
  419.4 10.7 %collective-permute-done.44 = bf16[64,2176]{1,0:T(8,128)(2,1)S(1)} collective-permute-done((bf16[64,2176]{1,0:T(8,128)(2,1)S(1)}, bf16[64,2176]{1,0:T(8,128)(2,1)S(1)}, u32[]{:S(2)}, u32[]{:S(2)}) %collective-permute-start.44) | collective-permute-done | bytes 278560 | tf_op jit(solution)/shard_map/ppermute | solution.py:660
  (222 shorter events, 83.3 us)
Async XLA Ops:
  1.5 7.8 %collective-permute-start = (bf16[2,16,1024]{2,1,0:T(8,128)(2,1)S(1)}, bf16[2,16,1024]{2,1,0:T(8,128)(2,1)S(1)}, u32[]{:S(2)}, u32[]{:S(2)}) collective-permute-start(bf16[2,16,1024]{2,1,0:T(8,128)(2,1)S(1)} %slice.282), channel_id=1, source_target_pairs={{0,2},{2,4},{4,6},{6,8},{8,10},{10,12},{12,14},{14,16},{16,18},{18... | collective-permute-start | bytes 196616 | tf_op jit(solution)/shard_map/ppermute | solution.py:676
  31.7 12.8 %collective-permute-start.1 = (bf16[4,144,384]{2,1,0:T(8,128)(2,1)}, bf16[4,144,384]{2,1,0:T(8,128)(2,1)S(1)}, u32[]{:S(2)}, u32[]{:S(2)}) collective-permute-start(bf16[4,144,384]{2,1,0:T(8,128)(2,1)} %bitcast.112), channel_id=1, source_target_pairs={{0,2},{2,4},{4,6},{6,8},{8,10},{10,12},{12,14},{14,16},{16,18},{18... | collective-permute-start | bytes 1327112 | tf_op jit(solution)/shard_map/ppermute | solution.py:676
  48.0 15.1 %collective-permute-start.2 = (bf16[4,144,384]{2,1,0:T(8,128)(2,1)}, bf16[4,144,384]{2,1,0:T(8,128)(2,1)S(1)}, u32[]{:S(2)}, u32[]{:S(2)}) collective-permute-start(bf16[4,144,384]{2,1,0:T(8,128)(2,1)} %get-tuple-element.95), channel_id=1, source_target_pairs={{0,4},{2,6},{4,8},{6,10},{8,12},{10,14},{12,16},{14,18},{16,20},{1... | collective-permute-start | bytes 1327112 | tf_op jit(solution)/shard_map/ppermute | solution.py:676
  53.2 7.2 %collective-permute-start.3 = (bf16[4,144,128]{2,1,0:T(8,128)(2,1)}, bf16[4,144,128]{2,1,0:T(8,128)(2,1)S(1)}, u32[]{:S(2)}, u32[]{:S(2)}) collective-permute-start(bf16[4,144,128]{2,1,0:T(8,128)(2,1)} %bitcast.114), channel_id=1, source_target_pairs={{2,0},{4,2},{6,4},{8,6},{10,8},{12,10},{14,12},{16,14},{18,16},{20... | collective-permute-start | bytes 442376 | tf_op jit(solution)/shard_map/ppermute | solution.py:676
  66.6 14.5 %collective-permute-start.4 = (bf16[4,144,384]{2,1,0:T(8,128)(2,1)}, bf16[4,144,384]{2,1,0:T(8,128)(2,1)S(1)}, u32[]{:S(2)}, u32[]{:S(2)}) collective-permute-start(bf16[4,144,384]{2,1,0:T(8,128)(2,1)} %get-tuple-element.102), channel_id=1, source_target_pairs={{0,8},{2,10},{4,12},{6,14},{8,16},{10,18},{12,20},{14,22},{16,24},... | collective-permute-start | bytes 1327112 | tf_op jit(solution)/shard_map/ppermute | solution.py:676
  71.2 7.2 %collective-permute-start.5 = (bf16[4,144,128]{2,1,0:T(8,128)(2,1)}, bf16[4,144,128]{2,1,0:T(8,128)(2,1)S(1)}, u32[]{:S(2)}, u32[]{:S(2)}) collective-permute-start(bf16[4,144,128]{2,1,0:T(8,128)(2,1)} %get-tuple-element.98), channel_id=1, source_target_pairs={{4,0},{6,2},{8,4},{10,6},{12,8},{14,10},{16,12},{18,14},{20,16},{2... | collective-permute-start | bytes 442376 | tf_op jit(solution)/shard_map/ppermute | solution.py:676
  84.6 18.6 %collective-permute-start.6 = (bf16[4,144,384]{2,1,0:T(8,128)(2,1)}, bf16[4,144,384]{2,1,0:T(8,128)(2,1)S(1)}, u32[]{:S(2)}, u32[]{:S(2)}) collective-permute-start(bf16[4,144,384]{2,1,0:T(8,128)(2,1)} %get-tuple-element.107), channel_id=1, source_target_pairs={{0,2},{2,4},{4,6},{6,8},{8,10},{10,12},{12,14},{14,16},{16,18},{18... | collective-permute-start | bytes 1327112 | tf_op jit(solution)/shard_map/ppermute | solution.py:676
  89.8 13.5 %collective-permute-start.7 = (bf16[4,128,256]{2,1,0:T(8,128)(2,1)}, bf16[4,128,256]{2,1,0:T(8,128)(2,1)S(1)}, u32[]{:S(2)}, u32[]{:S(2)}) collective-permute-start(bf16[4,128,256]{2,1,0:T(8,128)(2,1)} %get-tuple-element.108), channel_id=1, source_target_pairs={{0,18},{2,20},{4,22},{6,24},{8,26},{10,28},{12,30},{1,19},{3,21},{... | collective-permute-start | bytes 786440 | tf_op jit(solution)/shard_map/ppermute | solution.py:676
  93.4 7.2 %collective-permute-start.8 = (bf16[4,144,128]{2,1,0:T(8,128)(2,1)}, bf16[4,144,128]{2,1,0:T(8,128)(2,1)S(1)}, u32[]{:S(2)}, u32[]{:S(2)}) collective-permute-start(bf16[4,144,128]{2,1,0:T(8,128)(2,1)} %get-tuple-element.105), channel_id=1, source_target_pairs={{8,0},{10,2},{12,4},{14,6},{16,8},{18,10},{20,12},{22,14},{24,16},... | collective-permute-start | bytes 442376 | tf_op jit(solution)/shard_map/ppermute | solution.py:676
  112.1 2.9 collective-permute-start.9
  116.0 18.0 %copy-start.32 = (s32[16]{0:T(128)S(1)}, s32[16]{0:T(128)}, u32[]{:S(2)}) copy-start(s32[16]{0:T(128)} %constant.20.clone) | copy-start | bytes 196
  116.0 18.5 %copy-start.31 = (s32[16]{0:T(128)S(1)}, s32[16]{0:T(128)}, u32[]{:S(2)}) copy-start(s32[16]{0:T(128)} %constant.21.clone) | copy-start | bytes 196
  133.4 28.3 %collective-permute-start.12 = (bf16[2,256,1024]{2,1,0:T(8,128)(2,1)}, bf16[2,256,1024]{2,1,0:T(8,128)(2,1)S(1)}, u32[]{:S(2)}, u32[]{:S(2)}) collective-permute-start(bf16[2,256,1024]{2,1,0:T(8,128)(2,1)} %get-tuple-element.124.mine_ref), channel_id=1, source_target_pairs={{0,1},{1,0},{2,3},{3,2},{4,5},{5,4},{6,7},{7,6},{8,9},{9,8},{10,11... | collective-permute-start | bytes 3145736 | tf_op jit(solution)/shard_map/ppermute | solution.py:681
  133.6 45.6 %collective-permute-start.10 = (bf16[2,256,1024]{2,1,0:T(8,128)(2,1)}, bf16[2,256,1024]{2,1,0:T(8,128)(2,1)}, u32[]{:S(2)}, u32[]{:S(2)}) collective-permute-start(bf16[2,256,1024]{2,1,0:T(8,128)(2,1)} %get-tuple-element.120), channel_id=1, source_target_pairs={{0,1},{1,0},{2,3},{3,2},{4,5},{5,4},{6,7},{7,6},{8,9},{9,8},{10,11... | collective-permute-start | bytes 3145736 | tf_op jit(solution)/shard_map/ppermute | solution.py:681
  140.6 160.4 %collective-permute-start.41 = (bf16[512,2176]{1,0:T(8,128)(2,1)}, bf16[512,2176]{1,0:T(8,128)(2,1)S(1)}, u32[]{:S(2)}, u32[]{:S(2)}) collective-permute-start(bf16[512,2176]{1,0:T(8,128)(2,1)} %feed_a_send.1), channel_id=1, source_target_pairs={{0,2},{2,0},{4,6},{6,4},{8,10},{10,8},{12,14},{14,12},{16,18},{18,... | collective-permute-start | bytes 6684680 | tf_op jit(solution)/shard_map/ppermute | solution.py:660
  147.7 115.0 %collective-permute-start.45 = (bf16[512,2048]{1,0:T(8,128)(2,1)}, bf16[512,2048]{1,0:T(8,128)(2,1)S(1)}, u32[]{:S(2)}, u32[]{:S(2)}) collective-permute-start(bf16[512,2048]{1,0:T(8,128)(2,1)} %feed_b_send.1), channel_id=1, source_target_pairs={{0,4},{2,6},{4,0},{6,2},{8,12},{10,14},{12,8},{14,10},{16,20},{18,... | collective-permute-start | bytes 6291464 | tf_op jit(solution)/shard_map/ppermute | solution.py:660
  170.1 27.6 %collective-permute-start.13 = (bf16[4,128,256]{2,1,0:T(8,128)(2,1)}, bf16[4,128,256]{2,1,0:T(8,128)(2,1)S(1)}, u32[]{:S(2)}, u32[]{:S(2)}) collective-permute-start(bf16[4,128,256]{2,1,0:T(8,128)(2,1)} %bitcast.113), channel_id=1, source_target_pairs={{2,0},{4,2},{6,4},{8,6},{10,8},{12,10},{14,12},{16,14},{18,16},{20... | collective-permute-start | bytes 786440 | tf_op jit(solution)/shard_map/ppermute | solution.py:676
  171.7 8.8 %copy-start.1 = (f32[2,256,1024]{2,1,0:T(8,128)S(1)}, f32[2,256,1024]{2,1,0:T(8,128)}, u32[]{:S(2)}) copy-start(f32[2,256,1024]{2,1,0:T(8,128)} %get-tuple-element.119.resid_ref) | copy-start | bytes 6291460
  171.7 8.8 %copy-start.8 = (bf16[2,256,1024]{2,1,0:T(8,128)(2,1)S(1)}, bf16[2,256,1024]{2,1,0:T(8,128)(2,1)}, u32[]{:S(2)}) copy-start(bf16[2,256,1024]{2,1,0:T(8,128)(2,1)} %get-tuple-element.120) | copy-start | bytes 3145732
  174.5 36.6 %collective-permute-start.28 = (bf16[512,512]{1,0:T(8,128)(2,1)}, bf16[512,512]{1,0:T(8,128)(2,1)}, u32[]{:S(2)}, u32[]{:S(2)}) collective-permute-start(bf16[512,512]{1,0:T(8,128)(2,1)} %outgate_send.1), channel_id=1, source_target_pairs={{0,4},{2,6},{4,0},{6,2},{8,12},{10,14},{12,8},{14,10},{16,20},{18,... | collective-permute-start | bytes 1572872 | tf_op jit(solution)/shard_map/ppermute | solution.py:660
  179.2 39.3 %collective-permute-start.37 = (bf16[512,512]{1,0:T(8,128)(2,1)}, bf16[512,512]{1,0:T(8,128)(2,1)S(1)}, u32[]{:S(2)}, u32[]{:S(2)}) collective-permute-start(bf16[512,512]{1,0:T(8,128)(2,1)} %out_grad_send.1), channel_id=1, source_target_pairs={{0,2},{2,0},{4,6},{6,4},{8,10},{10,8},{12,14},{14,12},{16,18},{18,... | collective-permute-start | bytes 1572872 | tf_op jit(solution)/shard_map/ppermute | solution.py:660
  194.8 17.5 %copy-start.7 = (f32[512,512]{1,0:T(8,128)S(1)}, f32[512,512]{1,0:T(8,128)}, u32[]{:S(2)}) copy-start(f32[512,512]{1,0:T(8,128)} %outgate_keep.1) | copy-start | bytes 3145732
  200.8 20.6 %collective-permute-start.14 = (bf16[4,128,256]{2,1,0:T(8,128)(2,1)}, bf16[4,128,256]{2,1,0:T(8,128)(2,1)S(1)}, u32[]{:S(2)}, u32[]{:S(2)}) collective-permute-start(bf16[4,128,256]{2,1,0:T(8,128)(2,1)} %get-tuple-element.129), channel_id=1, source_target_pairs={{4,0},{6,2},{8,4},{10,6},{12,8},{14,10},{16,12},{18,14},{20,16},{2... | collective-permute-start | bytes 786440 | tf_op jit(solution)/shard_map/ppermute | solution.py:676
  212.3 6.4 %copy-start.6 = (f32[512,512]{1,0:T(8,128)S(1)}, f32[512,512]{1,0:T(8,128)}, u32[]{:S(2)}) copy-start(f32[512,512]{1,0:T(8,128)} %out_grad_keep.1) | copy-start | bytes 3145732
  212.5 13.3 %collective-permute-start.29 = (bf16[256,512]{1,0:T(8,128)(2,1)S(1)}, bf16[256,512]{1,0:T(8,128)(2,1)S(1)}, u32[]{:S(2)}, u32[]{:S(2)}) collective-permute-start(bf16[256,512]{1,0:T(8,128)(2,1)S(1)} %get-tuple-element.175), channel_id=1, source_target_pairs={{0,2},{2,0},{4,6},{6,4},{8,10},{10,8},{12,14},{14,12},{16,18},{18,... | collective-permute-start | bytes 786440 | tf_op jit(solution)/shard_map/ppermute | solution.py:660
  218.9 9.8 %collective-permute-start.38 = (bf16[256,512]{1,0:T(8,128)(2,1)S(1)}, bf16[256,512]{1,0:T(8,128)(2,1)S(1)}, u32[]{:S(2)}, u32[]{:S(2)}) collective-permute-start(bf16[256,512]{1,0:T(8,128)(2,1)S(1)} %get-tuple-element.173), channel_id=1, source_target_pairs={{0,4},{2,6},{4,0},{6,2},{8,12},{10,14},{12,8},{14,10},{16,20},{18,... | collective-permute-start | bytes 786440 | tf_op jit(solution)/shard_map/ppermute | solution.py:660
  224.6 11.3 %collective-permute-start.15 = (bf16[4,128,256]{2,1,0:T(8,128)(2,1)}, bf16[4,128,256]{2,1,0:T(8,128)(2,1)S(1)}, u32[]{:S(2)}, u32[]{:S(2)}) collective-permute-start(bf16[4,128,256]{2,1,0:T(8,128)(2,1)} %get-tuple-element.131), channel_id=1, source_target_pairs={{8,0},{10,2},{12,4},{14,6},{16,8},{18,10},{20,12},{22,14},{24,16},... | collective-permute-start | bytes 786440 | tf_op jit(solution)/shard_map/ppermute | solution.py:676
  226.0 14.4 %collective-permute-start.30 = (bf16[128,512]{1,0:T(8,128)(2,1)S(1)}, bf16[128,512]{1,0:T(8,128)(2,1)S(1)}, u32[]{:S(2)}, u32[]{:S(2)}) collective-permute-start(bf16[128,512]{1,0:T(8,128)(2,1)S(1)} %get-tuple-element.183), channel_id=1, source_target_pairs={{0,8},{2,10},{4,12},{6,14},{8,0},{10,2},{12,4},{14,6},{16,24},{18,... | collective-permute-start | bytes 393224 | tf_op jit(solution)/shard_map/ppermute | solution.py:660
  228.8 32.0 %copy-start.27 = (bf16[4,144,128]{2,1,0:T(8,128)(2,1)S(1)}, bf16[4,144,128]{2,1,0:T(8,128)(2,1)}, u32[]{:S(2)}) copy-start(bf16[4,144,128]{2,1,0:T(8,128)(2,1)} %get-tuple-element.111) | copy-start | bytes 442372
  228.9 12.9 %collective-permute-start.39 = (bf16[128,512]{1,0:T(8,128)(2,1)S(1)}, bf16[128,512]{1,0:T(8,128)(2,1)S(1)}, u32[]{:S(2)}, u32[]{:S(2)}) collective-permute-start(bf16[128,512]{1,0:T(8,128)(2,1)S(1)} %get-tuple-element.181), channel_id=1, source_target_pairs={{0,8},{2,10},{4,12},{6,14},{8,0},{10,2},{12,4},{14,6},{16,24},{18,... | collective-permute-start | bytes 393224 | tf_op jit(solution)/shard_map/ppermute | solution.py:660
  239.1 28.8 %collective-permute-start.16 = (bf16[4,128,256]{2,1,0:T(8,128)(2,1)}, bf16[4,128,256]{2,1,0:T(8,128)(2,1)S(1)}, u32[]{:S(2)}, u32[]{:S(2)}) collective-permute-start(bf16[4,128,256]{2,1,0:T(8,128)(2,1)} %get-tuple-element.132), channel_id=1, source_target_pairs={{2,0},{4,2},{6,4},{8,6},{10,8},{12,10},{14,12},{16,14},{18,16},{20... | collective-permute-start | bytes 786440 | tf_op jit(solution)/shard_map/ppermute | solution.py:676
  240.4 27.5 %collective-permute-start.17 = (bf16[4,128,256]{2,1,0:T(8,128)(2,1)}, bf16[4,128,256]{2,1,0:T(8,128)(2,1)S(1)}, u32[]{:S(2)}, u32[]{:S(2)}) collective-permute-start(bf16[4,128,256]{2,1,0:T(8,128)(2,1)} %get-tuple-element.132), channel_id=1, source_target_pairs={{18,0},{20,2},{22,4},{24,6},{26,8},{28,10},{30,12},{19,1},{21,3},{... | collective-permute-start | bytes 786440 | tf_op jit(solution)/shard_map/ppermute | solution.py:676
  241.7 13.9 %collective-permute-start.31 = (bf16[64,512]{1,0:T(8,128)(2,1)S(1)}, bf16[64,512]{1,0:T(8,128)(2,1)S(1)}, u32[]{:S(2)}, u32[]{:S(2)}) collective-permute-start(bf16[64,512]{1,0:T(8,128)(2,1)S(1)} %fusion.21), channel_id=1, source_target_pairs={{0,16},{2,18},{4,20},{6,22},{8,24},{10,26},{12,28},{14,30},{16,0},... | collective-permute-start | bytes 196616 | tf_op jit(solution)/shard_map/ppermute | solution.py:660
  255.6 5.2 %collective-permute-start.40 = (bf16[64,512]{1,0:T(8,128)(2,1)S(1)}, bf16[64,512]{1,0:T(8,128)(2,1)S(1)}, u32[]{:S(2)}, u32[]{:S(2)}) collective-permute-start(bf16[64,512]{1,0:T(8,128)(2,1)S(1)} %fusion.18), channel_id=1, source_target_pairs={{0,16},{2,18},{4,20},{6,22},{8,24},{10,26},{12,28},{14,30},{16,0},... | collective-permute-start | bytes 196616 | tf_op jit(solution)/shard_map/ppermute | solution.py:660
  260.8 7.1 %collective-permute-start.11 = (bf16[4,144,128]{2,1,0:T(8,128)(2,1)S(1)}, bf16[4,144,128]{2,1,0:T(8,128)(2,1)S(1)}, u32[]{:S(2)}, u32[]{:S(2)}) collective-permute-start(bf16[4,144,128]{2,1,0:T(8,128)(2,1)S(1)} %copy-done.27), channel_id=1, source_target_pairs={{2,0},{4,2},{6,4},{8,6},{10,8},{12,10},{14,12},{16,14},{18,16},{20... | collective-permute-start | bytes 442376 | tf_op jit(solution)/shard_map/ppermute | solution.py:676
  271.6 13.4 %copy-start = (f32[512,2048]{1,0:T(8,128)S(1)}, f32[512,2048]{1,0:T(8,128)}, u32[]{:S(2)}) copy-start(f32[512,2048]{1,0:T(8,128)} %feed_b_keep.1) | copy-start | bytes 12582916
  283.4 10.0 %copy-start.23 = (f32[4,768]{1,0:T(4,128)S(1)}, f32[4,768]{1,0:T(4,128)}, u32[]{:S(2)}) copy-start(f32[4,768]{1,0:T(4,128)} %get-tuple-element.151) | copy-start | bytes 36868
  283.4 10.0 %collective-permute-start.18 = (f32[2,16,1024]{2,1,0:T(8,128)S(1)}, f32[2,16,1024]{2,1,0:T(8,128)S(1)}, u32[]{:S(2)}, u32[]{:S(2)}) collective-permute-start(f32[2,16,1024]{2,1,0:T(8,128)S(1)} %slice.283), channel_id=1, source_target_pairs={{2,0},{4,2},{6,4},{8,6},{10,8},{12,10},{14,12},{16,14},{18,16},{20... | collective-permute-start | bytes 393224 | tf_op jit(solution)/shard_map/ppermute | solution.py:676
  285.0 18.0 %slice-start = ((s8[4456448]{0:T(1024)(128)(4,1)}), s8[262144]{0:T(1024)(128)(4,1)S(1)}, s32[]{:S(2)}) async-start(s8[4456448]{0:T(1024)(128)(4,1)} %bitcast.63), calls=%async_computation | async-start | bytes 524288
  289.7 81.6 %collective-permute-start.46 = (bf16[256,2048]{1,0:T(8,128)(2,1)}, bf16[256,2048]{1,0:T(8,128)(2,1)}, u32[]{:S(2)}, u32[]{:S(2)}) collective-permute-start(bf16[256,2048]{1,0:T(8,128)(2,1)} %get-tuple-element.165), channel_id=1, source_target_pairs={{0,2},{2,0},{4,6},{6,4},{8,10},{10,8},{12,14},{14,12},{16,18},{18,... | collective-permute-start | bytes 3145736 | tf_op jit(solution)/shard_map/ppermute | solution.py:660
  294.1 6.1 %copy-start.25 = (f32[1,256]{1,0:T(1,128)S(1)}, f32[1,256]{1,0:T(1,128)}, u32[]{:S(2)}) copy-start(f32[1,256]{1,0:T(1,128)} %get-tuple-element.153) | copy-start | bytes 3076
  294.1 6.8 %copy-start.33 = (f32[1,128]{1,0:T(1,128)S(1)}, f32[1,128]{1,0:T(1,128)}, u32[]{:S(2)}) copy-start(f32[1,128]{1,0:T(1,128)} %get-tuple-element.152) | copy-start | bytes 1540
  294.1 8.9 %slice-start.1 = ((s8[4456448]{0:T(1024)(128)(4,1)}), s8[4194304]{0:T(1024)(128)(4,1)S(1)}, s32[]{:S(2)}) async-start(s8[4456448]{0:T(1024)(128)(4,1)} %bitcast.63), calls=%async_computation.1 | async-start | bytes 8388608
  300.9 1.2 collective-permute-start.32
  302.1 12.3 %collective-permute-start.33 = (f32[51,128]{1,0:T(8,128)S(1)}, f32[51,128]{1,0:T(8,128)S(1)}, u32[]{:S(2)}, u32[]{:S(2)}) collective-permute-start(f32[51,128]{1,0:T(8,128)S(1)} %bitcast.93), channel_id=1, source_target_pairs={{0,2},{2,0},{4,6},{6,4},{8,10},{10,8},{12,14},{14,12},{16,18},{18,... | collective-permute-start | bytes 78344 | tf_op jit(solution)/shard_map/ppermute | solution.py:660
  304.6 88.4 %collective-permute-start.42 = (bf16[256,2176]{1,0:T(8,128)(2,1)}, bf16[256,2176]{1,0:T(8,128)(2,1)}, u32[]{:S(2)}, u32[]{:S(2)}) collective-permute-start(bf16[256,2176]{1,0:T(8,128)(2,1)} %get-tuple-element.163), channel_id=1, source_target_pairs={{0,4},{2,6},{4,0},{6,2},{8,12},{10,14},{12,8},{14,10},{16,20},{18,... | collective-permute-start | bytes 3342344 | tf_op jit(solution)/shard_map/ppermute | solution.py:660
  314.4 20.3 %collective-permute-start.34 = (f32[51,128]{1,0:T(8,128)S(1)}, f32[51,128]{1,0:T(8,128)S(1)}, u32[]{:S(2)}, u32[]{:S(2)}) collective-permute-start(f32[51,128]{1,0:T(8,128)S(1)} %bitcast_add_fusion), channel_id=1, source_target_pairs={{0,4},{2,6},{4,0},{6,2},{8,12},{10,14},{12,8},{14,10},{16,20},{18,... | collective-permute-start | bytes 78344 | tf_op jit(solution)/shard_map/ppermute | solution.py:660
  334.7 6.1 %collective-permute-start.35 = (f32[51,128]{1,0:T(8,128)S(1)}, f32[51,128]{1,0:T(8,128)S(1)}, u32[]{:S(2)}, u32[]{:S(2)}) collective-permute-start(f32[51,128]{1,0:T(8,128)S(1)} %fusion.26), channel_id=1, source_target_pairs={{0,8},{2,10},{4,12},{6,14},{8,0},{10,2},{12,4},{14,6},{16,24},{18,... | collective-permute-start | bytes 78344 | tf_op jit(solution)/shard_map/ppermute | solution.py:660
  340.9 6.2 %collective-permute-start.36 = (f32[51,128]{1,0:T(8,128)S(1)}, f32[51,128]{1,0:T(8,128)S(1)}, u32[]{:S(2)}, u32[]{:S(2)}) collective-permute-start(f32[51,128]{1,0:T(8,128)S(1)} %add.181), channel_id=1, source_target_pairs={{0,16},{2,18},{4,20},{6,22},{8,24},{10,26},{12,28},{14,30},{16,0},... | collective-permute-start | bytes 78344 | tf_op jit(solution)/shard_map/ppermute | solution.py:660
  343.8 45.2 %collective-permute-start.19 = (bf16[2,256,1024]{2,1,0:T(8,128)(2,1)}, bf16[2,256,1024]{2,1,0:T(8,128)(2,1)}, u32[]{:S(2)}, u32[]{:S(2)}) collective-permute-start(bf16[2,256,1024]{2,1,0:T(8,128)(2,1)} %get-tuple-element.146.mine_ref), channel_id=1, source_target_pairs={{0,1},{1,0},{2,3},{3,2},{4,5},{5,4},{6,7},{7,6},{8,9},{9,8},{10,11... | collective-permute-start | bytes 3145736 | tf_op jit(solution)/shard_map/ppermute | solution.py:681
  343.8 20.9 %collective-permute-start.20 = (bf16[512,640]{1,0:T(8,128)(2,1)}, bf16[512,640]{1,0:T(8,128)(2,1)}, u32[]{:S(2)}, u32[]{:S(2)}) collective-permute-start(bf16[512,640]{1,0:T(8,128)(2,1)} %query_key_send.1), channel_id=1, source_target_pairs={{0,2},{2,0},{4,6},{6,4},{8,10},{10,8},{12,14},{14,12},{16,18},{18,... | collective-permute-start | bytes 1966088 | tf_op jit(solution)/shard_map/ppermute | solution.py:660
  347.0 15.6 %copy-start.5 = (f32[512,512]{1,0:T(8,128)S(1)}, f32[512,512]{1,0:T(8,128)}, u32[]{:S(2)}) copy-start(f32[512,512]{1,0:T(8,128)} %value_keep.1) | copy-start | bytes 3145732
  347.0 14.4 %collective-permute-start.24 = (bf16[512,512]{1,0:T(8,128)(2,1)}, bf16[512,512]{1,0:T(8,128)(2,1)}, u32[]{:S(2)}, u32[]{:S(2)}) collective-permute-start(bf16[512,512]{1,0:T(8,128)(2,1)} %value_send.1), channel_id=1, source_target_pairs={{0,4},{2,6},{4,0},{6,2},{8,12},{10,14},{12,8},{14,10},{16,20},{18,... | collective-permute-start | bytes 1572872 | tf_op jit(solution)/shard_map/ppermute | solution.py:660
  362.8 7.7 %collective-permute-start.25 = (bf16[256,512]{1,0:T(8,128)(2,1)S(1)}, bf16[256,512]{1,0:T(8,128)(2,1)S(1)}, u32[]{:S(2)}, u32[]{:S(2)}) collective-permute-start(bf16[256,512]{1,0:T(8,128)(2,1)S(1)} %get-tuple-element.177), channel_id=1, source_target_pairs={{0,2},{2,0},{4,6},{6,4},{8,10},{10,8},{12,14},{14,12},{16,18},{18,... | collective-permute-start | bytes 786440 | tf_op jit(solution)/shard_map/ppermute | solution.py:660
  366.0 13.5 %collective-permute-start.21 = (bf16[256,640]{1,0:T(8,128)(2,1)S(1)}, bf16[256,640]{1,0:T(8,128)(2,1)S(1)}, u32[]{:S(2)}, u32[]{:S(2)}) collective-permute-start(bf16[256,640]{1,0:T(8,128)(2,1)S(1)} %get-tuple-element.171), channel_id=1, source_target_pairs={{0,4},{2,6},{4,0},{6,2},{8,12},{10,14},{12,8},{14,10},{16,20},{18,... | collective-permute-start | bytes 983048 | tf_op jit(solution)/shard_map/ppermute | solution.py:660
  370.7 5.7 %collective-permute-start.26 = (bf16[128,512]{1,0:T(8,128)(2,1)S(1)}, bf16[128,512]{1,0:T(8,128)(2,1)S(1)}, u32[]{:S(2)}, u32[]{:S(2)}) collective-permute-start(bf16[128,512]{1,0:T(8,128)(2,1)S(1)} %get-tuple-element.185), channel_id=1, source_target_pairs={{0,8},{2,10},{4,12},{6,14},{8,0},{10,2},{12,4},{14,6},{16,24},{18,... | collective-permute-start | bytes 393224 | tf_op jit(solution)/shard_map/ppermute | solution.py:660
  373.9 28.3 %collective-permute-start.47 = (bf16[128,2048]{1,0:T(8,128)(2,1)}, bf16[128,2048]{1,0:T(8,128)(2,1)}, u32[]{:S(2)}, u32[]{:S(2)}) collective-permute-start(bf16[128,2048]{1,0:T(8,128)(2,1)} %get-tuple-element.169), channel_id=1, source_target_pairs={{0,8},{2,10},{4,12},{6,14},{8,0},{10,2},{12,4},{14,6},{16,24},{18,... | collective-permute-start | bytes 1572872 | tf_op jit(solution)/shard_map/ppermute | solution.py:660
  376.5 11.8 %collective-permute-start.27 = (bf16[64,512]{1,0:T(8,128)(2,1)S(1)}, bf16[64,512]{1,0:T(8,128)(2,1)S(1)}, u32[]{:S(2)}, u32[]{:S(2)}) collective-permute-start(bf16[64,512]{1,0:T(8,128)(2,1)S(1)} %fusion.23), channel_id=1, source_target_pairs={{0,16},{2,18},{4,20},{6,22},{8,24},{10,26},{12,28},{14,30},{16,0},... | collective-permute-start | bytes 196616 | tf_op jit(solution)/shard_map/ppermute | solution.py:660
  379.6 14.8 %collective-permute-start.22 = (bf16[128,640]{1,0:T(8,128)(2,1)S(1)}, bf16[128,640]{1,0:T(8,128)(2,1)S(1)}, u32[]{:S(2)}, u32[]{:S(2)}) collective-permute-start(bf16[128,640]{1,0:T(8,128)(2,1)S(1)} %get-tuple-element.179), channel_id=1, source_target_pairs={{0,8},{2,10},{4,12},{6,14},{8,0},{10,2},{12,4},{14,6},{16,24},{18,... | collective-permute-start | bytes 491528 | tf_op jit(solution)/shard_map/ppermute | solution.py:660
  394.5 6.3 %collective-permute-start.23 = (bf16[64,640]{1,0:T(8,128)(2,1)S(1)}, bf16[64,640]{1,0:T(8,128)(2,1)S(1)}, u32[]{:S(2)}, u32[]{:S(2)}) collective-permute-start(bf16[64,640]{1,0:T(8,128)(2,1)S(1)} %fusion.16), channel_id=1, source_target_pairs={{0,16},{2,18},{4,20},{6,22},{8,24},{10,26},{12,28},{14,30},{16,0},... | collective-permute-start | bytes 245768 | tf_op jit(solution)/shard_map/ppermute | solution.py:660
  399.4 17.3 %collective-permute-start.43 = (bf16[128,2176]{1,0:T(8,128)(2,1)}, bf16[128,2176]{1,0:T(8,128)(2,1)S(1)}, u32[]{:S(2)}, u32[]{:S(2)}) collective-permute-start(bf16[128,2176]{1,0:T(8,128)(2,1)} %get-tuple-element.167), channel_id=1, source_target_pairs={{0,8},{2,10},{4,12},{6,14},{8,0},{10,2},{12,4},{14,6},{16,24},{18,... | collective-permute-start | bytes 1671176 | tf_op jit(solution)/shard_map/ppermute | solution.py:660
  402.2 14.7 %copy-start.4 = (f32[128,2176]{1,0:T(8,128)S(1)}, f32[128,2176]{1,0:T(8,128)}, u32[]{:S(2)}) copy-start(f32[128,2176]{1,0:T(8,128)} %get-tuple-element.166) | copy-start | bytes 3342340
  403.5 15.1 %collective-permute-start.48 = (bf16[64,2048]{1,0:T(8,128)(2,1)S(1)}, bf16[64,2048]{1,0:T(8,128)(2,1)S(1)}, u32[]{:S(2)}, u32[]{:S(2)}) collective-permute-start(bf16[64,2048]{1,0:T(8,128)(2,1)S(1)} %fusion.7), channel_id=1, source_target_pairs={{0,16},{2,18},{4,20},{6,22},{8,24},{10,26},{12,28},{14,30},{16,0},... | collective-permute-start | bytes 786440 | tf_op jit(solution)/shard_map/ppermute | solution.py:660
  416.9 13.2 %collective-permute-start.44 = (bf16[64,2176]{1,0:T(8,128)(2,1)S(1)}, bf16[64,2176]{1,0:T(8,128)(2,1)S(1)}, u32[]{:S(2)}, u32[]{:S(2)}) collective-permute-start(bf16[64,2176]{1,0:T(8,128)(2,1)S(1)} %fusion.5), channel_id=1, source_target_pairs={{0,16},{2,18},{4,20},{6,22},{8,24},{10,26},{12,28},{14,30},{16,0},... | collective-permute-start | bytes 835592 | tf_op jit(solution)/shard_map/ppermute | solution.py:660
  (21 other events, 20.3 us)
